TPU v7x, 256 devices: a whole 4x4x8 slice. The times are simulated.
256 devices in a mesh: row: 8 (over z_hi, y), col: 32 (over z_lo, x, core).
Axes of the slice: x: 4, y: 4, z: 8 (z_hi: 2, z_lo: 4; z = z_hi * 4 + z_lo), core: 2. Of those that a mesh axis runs over, the one named last changes fastest.
Arguments:
- sigma_anc: float32 [16384, 16384], P('row', 'col'), as said below
- factor: float32 [2048, 16384], P('col', 'row'), may hold values from -0.046875 to 0.046875
- pattern: int32 [8, 64], replicated, may hold values 0 or 1
- base_var: float32 [2048], P('col'), may hold values from 0.5 to 2
Outputs:
- sigma_off: float32 [2048, 16384], P('col', 'row')
- variances: float32 [2048], P('col')
Inputs may be any that keep to these rules, and one draw needn't show every extreme that they name: sigma_anc is exactly symmetric, with positive diagonal entries.
All inputs are finite; a program needn't handle non-finite values.
Results may differ from a plain program's by a relative error of at most 0.00007.
Values sent between devices are 32-bit elements; how exact they have to be, the bound alone decides.
No kernel may reach another device: no remote copies, remote signals or barrier semaphores. Data moves between devices by JAX's collectives and lax.ppermute only.
A program may use at most 64 MiB of HBM per device.

v0:
```python
import jax
import jax.numpy as jnp
from jax import lax
from jax.sharding import PartitionSpec as P

B = 256


def body(sigma_anc, factor, pattern, base_var):
    rows_here = factor.shape[0]
    cols_here = factor.shape[1]
    row_start = lax.axis_index("col") * rows_here
    col_start = lax.axis_index("row") * cols_here
    super_index = (row_start + jnp.arange(rows_here, dtype=jnp.int32)) // B
    block_index = (col_start + jnp.arange(cols_here, dtype=jnp.int32)) // B
    super_hot = (
        super_index[:, None] == jnp.arange(pattern.shape[0], dtype=jnp.int32)[None, :]
    ).astype(jnp.float32)
    block_hot = (
        block_index[:, None] == jnp.arange(pattern.shape[1], dtype=jnp.int32)[None, :]
    ).astype(jnp.float32)
    row_pattern = jnp.dot(
        super_hot,
        pattern.astype(jnp.float32),
        precision=lax.Precision.HIGHEST,
        preferred_element_type=jnp.float32,
    )
    mask = lax.dot_general(
        row_pattern,
        block_hot,
        (((1,), (1,)), ((), ())),
        precision=lax.Precision.HIGHEST,
        preferred_element_type=jnp.float32,
    )
    masked = factor * mask
    spread = lax.all_gather(masked, "row", axis=1, tiled=True)
    regrouped = lax.all_to_all(spread, "col", split_axis=1, concat_axis=0, tiled=True)
    product = lax.psum_scatter(
        lax.dot_general(
            regrouped,
            sigma_anc,
            (((1,), (1,)), ((), ())),
            precision=lax.Precision.HIGHEST,
            preferred_element_type=jnp.float32,
        ),
        "col",
        scatter_dimension=0,
        tiled=True,
    )
    sigma_off = -(product * mask)
    partial_var = jnp.sum(product * masked, axis=1)
    variances = base_var + lax.psum(partial_var, "row")
    return (sigma_off, variances)


def solution(mesh):
    in_specs = (P("row", "col"), P("col", "row"), P(), P("col"))
    out_specs = (P("col", "row"), P("col"))
    return jax.shard_map(body, mesh=mesh, in_specs=in_specs, out_specs=out_specs, check_vma=False)
```

profile of v0, /device:TPU:0, one launch (start us, length us, event | category | flops | bytes accessed | tf_op | source)
XLA Modules:
  0.0 457.3 jit_solution(8426645351663367905)
XLA Ops:
  7.2 0.0 all-gather.2.cloned.1.call-start
  7.3 0.9 fusion.2
  8.1 2.7 fusion.8
  10.9 0.0 all-gather.2.cloned.1.call-update
  10.9 0.0 reduce-scatter.2.cloned.1.call-start
  10.9 108.6 %all-gather.2.cloned.1.call-done = f32[64,16384]{1,0:T(8,128)} async-done(((f32[64,2048]{1,0:T(8,128)}), f32[64,16384]{1,0:T(8,128)}) %all-gather.2.cloned.1.call-update) | async-done | bytes 4194320 | tf_op jit(solution)/shard_map/all_gather | solution.py:36
  119.5 2.8 copy.9
  122.3 0.0 copy-start.1
  122.4 98.4 %all_to_all.19 = f32[64,32,512]{2,0,1:T(8,128)S(1)} all-to-all(f32[64,32,512]{2,0,1:T(8,128)S(1)} %bitcast.11), channel_id=1, replica_groups=mesh['row'=8,'col'=32] {'col'}, dimensions={1} | all-to-all | bytes 8388608 | tf_op jit(solution)/shard_map/all_to_all | solution.py:37
  220.7 0.0 copy-done.1
  220.7 29.6 %fusion.9 = f32[2048,2048]{1,0:T(8,128)} fusion(f32[2048,512]{1,0:T(8,128)S(1)} %bitcast.10, f32[2048,512]{1,0:T(8,128)S(1)} %copy-done.1), kind=kOutput, calls=%fused_computation.24 | convolution fusion | flops 25769803776 | bytes 25165824 | tf_op jit(solution)/shard_map/dot_general | solution.py:39
  250.4 0.0 copy-start
  250.4 0.0 copy-start.2
  250.4 0.0 reduce-scatter.2.cloned.1.call-update
  250.4 168.4 %reduce-scatter.2.cloned.1.call-done = f32[64,2048]{1,0:T(8,128)} async-done(((f32[2048,2048]{1,0:T(8,128)}), f32[64,2048]{1,0:T(8,128)}) %reduce-scatter.2.cloned.1.call-update) | async-done | bytes 524304 | tf_op jit(solution)/shard_map/reduce_scatter | solution.py:38
  418.8 0.0 copy-done
  418.8 2.0 multiply_reduce_fusion
  420.8 29.1 %psum.7 = f32[64]{0:T(128)S(1)} all-reduce(f32[64]{0:T(128)S(1)} %get-tuple-element.2), channel_id=1, replica_groups=mesh['row'=8,'col'=32] {'row'}, use_global_device_ids=true, to_apply=%region_2.3 | all-reduce | flops 64 | bytes 512 | tf_op jit(solution)/shard_map/psum | solution.py:52
  450.0 0.0 copy-done.2
  450.0 0.5 add.41
  (2 shorter events, 0.0 us)
Async XLA Ops:
  7.2 112.4 %all-gather.2.cloned.1.call-start = ((), (), s32[]{:S(2)}) async-start(), calls=%async_computation.2 | async-start | bytes 4718592 | tf_op jit(solution)/shard_map/all_gather | solution.py:36
  10.9 407.9 %reduce-scatter.2.cloned.1.call-start = ((), (), s32[]{:S(2)}) async-start(), calls=%async_computation.3 | async-start | bytes 17301504 | tf_op jit(solution)/shard_map/reduce_scatter | solution.py:38
  122.3 98.4 %copy-start.1 = (f32[2048,512]{1,0:T(8,128)S(1)}, f32[2048,512]{1,0:T(8,128)}, u32[]{:S(2)}) copy-start(f32[2048,512]{1,0:T(8,128)} %param.4) | copy-start | bytes 12582916
  250.4 168.5 %copy-start = (f32[64,2048]{1,0:T(8,128)S(1)}, f32[64,2048]{1,0:T(8,128)}, u32[]{:S(2)}) copy-start(f32[64,2048]{1,0:T(8,128)} %get-tuple-element.4) | copy-start | bytes 1572868
  250.4 199.6 %copy-start.2 = (f32[64]{0:T(128)S(1)}, f32[64]{0:T(128)}, u32[]{:S(2)}) copy-start(f32[64]{0:T(128)} %param.7) | copy-start | bytes 772
Sparse Core Ops, SparseCore 0:
  11.2 108.2 all-gather.1
  250.5 168.2 reduce-scatter.1
where the time goes:
time: 458 us; the launch traced here: 457 us
  waiting for transfers between devices  277 us (60%)
  blocking collectives  128 us (28%)
  matrix products  33.2 us (7%)
  between operations  14.1 us (3%)
    reduce_scatter x1, waiting for transfers between devices, body(): lax.psum_scatter(lax.dot_general(regrouped, sigma_anc, (((1,), (1,)), (()...  168 us
    all_gather x1, waiting for transfers between devices, body(): spread = lax.all_gather(masked, 'row', axis=1, tiled=True)  109 us
    all_to_all x1, blocking collectives, body(): lax.all_to_all(spread, 'col', split_axis=1, concat_axis=0, tiled=True)  98.4 us
    dot_general x1, matrix products, body(): lax.dot_general(regrouped, sigma_anc, (((1,), (1,)), ((), ())), precision...  29.6 us
    psum x1, blocking collectives, body(): variances = base_var + lax.psum(partial_var, 'row')  29.1 us
  transfers between devices with their start and end apart: 2, of which 2 were waited for; matrix products, arithmetic and copies ran while one was open for 0% of the time, Pallas kernels for 0%

commit v1 on v0

v1 whole, which is shorter than its diff:
```python
import jax
import jax.numpy as jnp
from jax import lax
from jax.experimental import pallas as pl
from jax.experimental.pallas import tpu as pltpu
from jax.sharding import PartitionSpec as P

B = 256
AXES = ("row", "col")
FIRST = 40
F32, BF16 = jnp.float32, jnp.bfloat16


def table(move):
    perm = []
    for i in range(256):
        zh, y, zl, x, k = i >> 7, (i >> 5) & 3, (i >> 3) & 3, (i >> 1) & 3, i & 1
        zh, y, zl, x, k = move(zh, y, zl, x, k)
        perm.append((i, (zh << 7) | ((y % 4) << 5) | ((zl % 4) << 3) | ((x % 4) << 1) | k))
    return perm


def along_x(n):
    return table(lambda zh, y, zl, x, k: (zh, y, zl, x + n, k))


def along_y(n):
    return table(lambda zh, y, zl, x, k: (zh, y + n, zl, x, k))


def along_zl(n):
    return table(lambda zh, y, zl, x, k: (zh, y, zl + n, x, k))


OTHER_ZH = table(lambda zh, y, zl, x, k: (1 - zh, y, zl, x, k))
OTHER_CORE = table(lambda zh, y, zl, x, k: (zh, y, zl, x, 1 - k))


def regroup(n):
    perm = []
    for i in range(256):
        r, c = i >> 5, i & 31
        perm.append((i, (c // 4) * 32 + 4 * r + (c + n) % 4))
    return perm


def send(value, perm):
    return lax.ppermute(value, AXES, perm)


def tie(*values):
    return lax.optimization_barrier(values)


def split(value):
    high = value.astype(BF16)
    return high, (value - high.astype(F32)).astype(BF16)


def split_kernel(value_ref, high_ref, low_ref):
    high_ref[...], low_ref[...] = split(value_ref[...])


def split_all(value):
    spec = pl.BlockSpec((256, value.shape[1]), lambda i: (i, 0))
    return pl.pallas_call(
        split_kernel,
        grid=(value.shape[0] // 256,),
        in_specs=[spec],
        out_specs=[spec] * 2,
        out_shape=[jax.ShapeDtypeStruct(value.shape, BF16)] * 2,
        name="split_sigma",
    )(value)


def whole_kernel(tab_ref, rows_ref, sh_ref, sl_ref, out_ref):
    step = pl.program_id(0)
    blocks, rows, depth = rows_ref.shape
    hi, lo = split(rows_ref[...].reshape(blocks * rows, depth))
    for n in range(0, out_ref.shape[2], 256):
        dot = lambda a, b: jnp.dot(a, b[:, n : n + 256], preferred_element_type=F32)
        acc = dot(lo, sh_ref) + dot(hi, sl_ref) + dot(hi, sh_ref)
        for b in range(blocks):
            out_ref[tab_ref[step * blocks + b], :, n : n + 256] = acc[b * rows : (b + 1) * rows]


def whole_products(tab, gathered, sigma):
    blocks, rows, depth = gathered.shape
    width = sigma[0].shape[1]
    group = 8
    whole = pl.BlockSpec(sigma[0].shape, lambda i: (0, 0))
    return pl.pallas_call(
        whole_kernel,
        grid=(blocks // group,),
        in_specs=[
            pl.BlockSpec(memory_space=pltpu.SMEM),
            pl.BlockSpec((group, rows, depth), lambda i: (i, 0, 0)),
            whole,
            whole,
        ],
        out_specs=pl.BlockSpec((blocks, rows, width), lambda i: (0, 0, 0)),
        out_shape=jax.ShapeDtypeStruct((blocks, rows, width), F32),
        compiler_params=pltpu.CompilerParams(vmem_limit_bytes=40 * 2**20),
        cost_estimate=pl.CostEstimate(
            flops=6 * blocks * rows * depth * width,
            bytes_accessed=blocks * rows * depth * 4 + 2**23,
            transcendentals=0,
        ),
        name="whole_products",
    )(tab, gathered, *sigma)


def turn_kernel(core_ref, own_ref, recv_ref, high_ref, low_ref):
    n = own_ref.shape[1]
    for at, ref in ((0, own_ref), (n, recv_ref)):
        high_ref[at : at + n, :], low_ref[at : at + n, :] = split(ref[...].T)


def turn_both(core, sigma, recv):
    rows, n = recv.shape
    steps = rows // 256
    return pl.pallas_call(
        turn_kernel,
        grid_spec=pltpu.PrefetchScalarGridSpec(
            num_scalar_prefetch=1,
            grid=(steps,),
            in_specs=[
                pl.BlockSpec((256, n), lambda i, core: (i + core[0] * steps, 0)),
                pl.BlockSpec((256, n), lambda i, core: (i, 0)),
            ],
            out_specs=[pl.BlockSpec((2 * n, 256), lambda i, core: (0, i))] * 2,
        ),
        out_shape=[jax.ShapeDtypeStruct((2 * n, rows), BF16)] * 2,
        name="turn_sigma",
    )(core, sigma, recv)


def turned_kernel(tab_ref, own_ref, recv_ref, sh_ref, sl_ref, *refs):
    outs, rows_ref = refs[:-1], refs[-1]
    blocks, rows, n = own_ref.shape
    for side, ref in ((0, own_ref), (1, recv_ref)):
        for b in range(blocks):
            at = pl.ds(pl.multiple_of(tab_ref[side, b] * rows, rows), rows)
            rows_ref[at, side * n : side * n + n] = ref[b]
    hi, lo = split(rows_ref[...])
    for c in range(0, sh_ref.shape[1], 256):
        columns = slice(c, c + 256)
        dot = lambda a, b: jnp.dot(a, b[:, columns], preferred_element_type=F32)
        acc = dot(lo, sh_ref) + dot(hi, sl_ref) + dot(hi, sh_ref)
        at = 0
        for out in outs:
            for b in range(out.shape[0]):
                out[b, :, columns] = acc[at : at + rows]
                at += rows


def turned_products(tab, own, recv, sigmas):
    blocks, rows, n = own.shape
    vmem = pl.BlockSpec(memory_space=pltpu.VMEM)
    total = blocks * rows
    width = sigmas[0].shape[1]
    return pl.pallas_call(
        turned_kernel,
        in_specs=[pl.BlockSpec(memory_space=pltpu.SMEM)] + [vmem] * 4,
        out_specs=[vmem] * 5,
        out_shape=[jax.ShapeDtypeStruct((n, rows, width), F32) for n in (8, 8, 4, 4, 8)],
        scratch_shapes=[pltpu.VMEM((total, 2 * n), F32)],
        compiler_params=pltpu.CompilerParams(vmem_limit_bytes=40 * 2**20),
        cost_estimate=pl.CostEstimate(
            flops=6 * total * 2 * n * width, bytes_accessed=total * 8192 + 2**22, transcendentals=0
        ),
        name="turned_products",
    )(tab, own, recv, *sigmas)


def final_kernel(shift_ref, mask_ref, masked_ref, *refs):
    blocks, halves, (off_ref, var_ref) = refs[:4], refs[4:6], refs[6:]
    at = 0
    for pieces, places, width in ((blocks, (0, 1, 2, 3), 512), (halves, (4, 5), 1024)):
        rows = pieces[0].shape[0]
        total = jnp.zeros((rows, 128), F32)
        for piece, k in zip(pieces, places):
            columns = pl.ds(pl.multiple_of(shift_ref[k] * width, width), width)
            product = piece[...]
            off_ref[at : at + rows, columns] = -(product * mask_ref[:, columns])
            part = product * masked_ref[at : at + rows, columns]
            for n in range(0, width, 128):
                total += part[:, n : n + 128]
        var_ref[at : at + rows, :] = total
        at += rows


def finish(shift, mask, masked, groups):
    vmem = pl.BlockSpec(memory_space=pltpu.VMEM)
    return pl.pallas_call(
        final_kernel,
        in_specs=[pl.BlockSpec(memory_space=pltpu.SMEM)] + [vmem] * (2 + len(groups)),
        out_specs=[vmem] * 2,
        out_shape=[
            jax.ShapeDtypeStruct(masked.shape, F32),
            jax.ShapeDtypeStruct((masked.shape[0], 128), F32),
        ],
        name="finish",
    )(shift, mask, masked, *groups)


def places(row, col):
    zh, y, zl, x, core = row // 4, row % 4, col // 8, (col // 2) % 4, col % 2
    c = jnp.arange(32, dtype=jnp.int32)
    s, i = c // 4, c % 4
    whole = (s % 4) * 8 + ((s // 4) ^ zh) * 4 + (i - col) % 4
    d, e, k = c // 8, (c // 4) % 2, c % 4
    s = (zh ^ e) * 4 + (y - d) % 4
    tabs = []
    for c in (col, col ^ 1):
        i = (c - k) % 4
        to_zl, to_x, to_core = s // 2, 2 * (s % 2) + i // 2, i % 2
        tabs.append(((to_x - x) % 4) * 8 + ((to_zl - zl) % 4) * 2 + (to_core ^ core))
    return whole, jnp.stack(tabs)


def body(sigma_anc, factor, pattern, base_var):
    row, col = lax.axis_index("row"), lax.axis_index("col")
    core = col % 2
    whole_tab, turned_tab = places(row, col)
    half = 1024
    blocks = lax.dynamic_slice(pattern, (col // 4, row * 8), (1, 8)).astype(F32)
    mask = jnp.repeat(blocks, B, axis=1)
    masked = factor * mask

    gathered = lax.all_gather(masked[:FIRST], "col")

    rest = masked[FIRST:]
    rows = rest.shape[0]
    quarters = [
        send(lax.dynamic_slice(rest, (0, 512 * ((col + n) % 4)), (rows, 512)), regroup(n))
        for n in range(4)
    ]
    own = to_other_zh(jnp.stack(quarters))
    own, sigma_anc = tie(own, sigma_anc)
    own = jnp.concatenate([own] + [send(own, along_y(n)) for n in (1, 2, 3)])
    sigma_other = lax.dynamic_slice(sigma_anc, ((1 - core) * half, 0), (half, 512))
    sigma = split_all(sigma_anc)
    turned = turn_both(core[None], sigma_anc, send(sigma_other, OTHER_CORE))
    own, sigma, turned = tie(own, sigma, turned)
    recv = send(own, OTHER_CORE)

    first = whole_products(whole_tab, gathered, sigma)
    first, recv = tie(first, recv)
    here, right, far_right, far_left, left = turned_products(turned_tab, own, recv, turned)
    pairs = [[0, 1, 2, 3], [4, 5, 6, 7]]
    first = lax.psum_scatter(first, "row", scatter_dimension=0, axis_index_groups=pairs, tiled=True)

    right = jnp.concatenate([right[:4] + send(far_right, along_x(1)), right[4:]])
    left = jnp.concatenate([left[:4], left[4:] + send(far_left, along_x(-1))])
    here = here + send(right, along_x(1)) + send(left, along_x(-1))
    first = sum_zh(first)
    here, first = tie(here, first)
    groups = [send(first[n], regroup(n)) for n in range(4)]
    total = here[:2]
    for n in (1, 2, 3):
        total = total + send(here[2 * n : 2 * n + 2], along_zl(n))
    *groups, total = tie(*groups, total)
    groups += [total[0], send(total[1], OTHER_CORE)]

    shift = jnp.concatenate([(col - jnp.arange(4, dtype=jnp.int32)) % 4, jnp.stack([core, 1 - core])])
    sigma_off, var_lanes = finish(shift, mask, masked, groups)
    part = jnp.sum(var_lanes, axis=1)
    shares = jnp.broadcast_to(part[None, :], (8, part.shape[0]))
    shares = lax.all_to_all(shares, "row", 0, 0, tiled=True)
    return sigma_off, base_var + jnp.sum(shares, axis=0)


def to_other_zh(part):
    return jnp.concatenate([part, send(part, OTHER_ZH)])


def sum_zh(part):
    return part[:4] + send(part[4:], OTHER_ZH)


def solution(mesh):
    in_specs = (P("row", "col"), P("col", "row"), P(), P("col"))
    out_specs = (P("col", "row"), P("col"))
    return jax.shard_map(body, mesh=mesh, in_specs=in_specs, out_specs=out_specs, check_vma=False)
```

time: 458 us -> 232 us (0.51)
  the two profiles are of different devices: /device:TPU:0 before, /device:TPU:36 now
where the time goes in v1:
time: 232 us; the launch traced here: 227 us
  waiting for transfers between devices  85.3 us (37%)
  starting transfers between devices  52.9 us (23%)
  Pallas kernels  32.1 us (14%)
  blocking collectives  20.4 us (9%)
  local copies, waits for them, and re-layouts  16.1 us (7%)
  between operations  14.5 us (6%)
  other arithmetic  5.7 us (2%)
    ppermute x23, waiting for transfers between devices, send(): return lax.ppermute(value, AXES, perm)  59.7 us
    ppermute x23, starting transfers between devices, send(): return lax.ppermute(value, AXES, perm)  52.8 us
    all_to_all x1, blocking collectives, body(): shares = lax.all_to_all(shares, 'row', 0, 0, tiled=True)  20.4 us
    all_gather x1, waiting for transfers between devices, body(): gathered = lax.all_gather(masked[:FIRST], 'col')  15 us
    pallas_call x1, Pallas kernels, whole_products(): pl.pallas_call(whole_kernel, grid=(blocks // group,), in_specs=[pl.BlockS...  12.2 us
    reduce_scatter x1, waiting for transfers between devices, body(): lax.psum_scatter(first, 'row', scatter_dimension=0, axis_index_groups=pai...  10.6 us
    unnamed x35, local copies, waits for them, and re-layouts  10.2 us
    pallas_call x1, Pallas kernels, split_all(): pl.pallas_call(split_kernel, grid=(value.shape[0] // 256,), in_specs=[spe...  6.75 us
  transfers between devices with their start and end apart: 25, of which 13 were waited for; matrix products, arithmetic and copies ran while one was open for 3% of the time, Pallas kernels for 13%

profile of v1, /device:TPU:36, one launch (start us, length us, event | category | flops | bytes accessed | tf_op | source)
XLA Modules:
  0.0 227.0 jit_solution(16688469026344513921)
XLA Ops:
  7.2 0.8 convert_bitcast_fusion
  8.0 0.1 broadcast_bitcast_fusion
  8.1 1.1 broadcast_multiply_fusion.masked_ref
  9.2 0.8 slice.73
  10.0 0.0 reduce-scatter.2.cloned.1.call-start
  10.2 2.0 collective-permute-start.3
  12.2 2.5 %collective-permute-start.2 = (f32[24,512]{1,0:T(8,128)S(1)}, f32[24,512]{1,0:T(8,128)S(1)}, u32[]{:S(2)}, u32[]{:S(2)}) collective-permute-start(f32[24,512]{1,0:T(8,128)S(1)} %get-tuple-element.70), channel_id=1, source_target_pairs={{0,2},{1,3},{2,0},{3,1},{4,34},{5,35},{6,32},{7,33},{8,66},{9,67},... | collective-permute-start | bytes 147464 | tf_op jit(solution)/shard_map/ppermute | solution.py:48
  14.7 4.6 %collective-permute-start.1 = (f32[24,512]{1,0:T(8,128)S(1)}, f32[24,512]{1,0:T(8,128)S(1)}, u32[]{:S(2)}, u32[]{:S(2)}) collective-permute-start(f32[24,512]{1,0:T(8,128)S(1)} %get-tuple-element.71), channel_id=1, source_target_pairs={{0,1},{1,2},{2,3},{3,0},{4,33},{5,34},{6,35},{7,32},{8,65},{9,66},... | collective-permute-start | bytes 147464 | tf_op jit(solution)/shard_map/ppermute | solution.py:48
  19.4 4.4 %collective-permute-start = (f32[24,512]{1,0:T(8,128)S(1)}, f32[24,512]{1,0:T(8,128)S(1)}, u32[]{:S(2)}, u32[]{:S(2)}) collective-permute-start(f32[24,512]{1,0:T(8,128)S(1)} %get-tuple-element.72), channel_id=1, source_target_pairs={{0,0},{1,1},{2,2},{3,3},{4,32},{5,33},{6,34},{7,35},{8,64},{9,65},... | collective-permute-start | bytes 147464 | tf_op jit(solution)/shard_map/ppermute | solution.py:48
  23.9 6.9 %collective-permute-done = f32[24,512]{1,0:T(8,128)S(1)} collective-permute-done((f32[24,512]{1,0:T(8,128)S(1)}, f32[24,512]{1,0:T(8,128)S(1)}, u32[]{:S(2)}, u32[]{:S(2)}) %collective-permute-start) | collective-permute-done | bytes 49184 | tf_op jit(solution)/shard_map/ppermute | solution.py:48
  30.8 12.5 %collective-permute-start.4 = (f32[4,24,512]{2,1,0:T(8,128)S(1)}, f32[4,24,512]{2,1,0:T(8,128)S(1)}, u32[]{:S(2)}, u32[]{:S(2)}) collective-permute-start(f32[4,24,512]{2,1,0:T(8,128)S(1)} %pad_maximum_fusion.3), channel_id=1, source_target_pairs={{0,128},{1,129},{2,130},{3,131},{4,132},{5,133},{6,134},{7,135},{8... | collective-permute-start | bytes 589832 | tf_op jit(solution)/shard_map/ppermute | solution.py:48
  43.3 6.1 %collective-permute-done.4 = f32[4,24,512]{2,1,0:T(8,128)S(1)} collective-permute-done((f32[4,24,512]{2,1,0:T(8,128)S(1)}, f32[4,24,512]{2,1,0:T(8,128)S(1)}, u32[]{:S(2)}, u32[]{:S(2)}) %collective-permute-start.4) | collective-permute-done | bytes 196640 | tf_op jit(solution)/shard_map/ppermute | solution.py:48
  49.4 3.2 %constant_dynamic-slice_fusion = f32[1024,512]{1,0:T(8,128)} fusion(f32[2048,512]{1,0:T(8,128)} %own_ref, s32[]{:T(128)S(6)} %select_n.341), kind=kLoop, calls=%fused_computation.63 | loop fusion | bytes 4194308 | tf_op jit(solution)/shard_map/dynamic_slice | solution.py:242
  52.7 0.1 collective-permute-start.6
  52.8 1.9 collective-permute-start.5
  54.7 6.8 %split_sigma.1 = (bf16[2048,512]{1,0:T(8,128)(2,1)}, bf16[2048,512]{1,0:T(8,128)(2,1)}) custom-call(f32[2048,512]{1,0:T(8,128)} %own_ref), custom_call_target="tpu_custom_call" | custom-call | tf_op jit(solution)/shard_map/split_sigma/pallas_call | solution.py:66
  61.5 3.1 %collective-permute-done.7 = f32[8,24,512]{2,1,0:T(8,128)S(1)} collective-permute-done((f32[8,24,512]{2,1,0:T(8,128)S(1)}, f32[8,24,512]{2,1,0:T(8,128)S(1)}, u32[]{:S(2)}, u32[]{:S(2)}) %collective-permute-start.7) | collective-permute-done | bytes 393248 | tf_op jit(solution)/shard_map/ppermute | solution.py:48
  64.6 1.7 collective-permute-done.6
  66.2 7.9 %collective-permute-done.5 = f32[8,24,512]{2,1,0:T(8,128)S(1)} collective-permute-done((f32[8,24,512]{2,1,0:T(8,128)S(1)}, f32[8,24,512]{2,1,0:T(8,128)S(1)}, u32[]{:S(2)}, u32[]{:S(2)}) %collective-permute-start.5) | collective-permute-done | bytes 393248 | tf_op jit(solution)/shard_map/ppermute | solution.py:48
  74.1 0.1 pad_maximum_fusion.own_ref
  74.3 5.3 %turn_sigma.1 = (bf16[1024,1024]{1,0:T(8,128)(2,1)}, bf16[1024,1024]{1,0:T(8,128)(2,1)}) custom-call(s32[1]{0:T(128)} %bitcast.core_ref, f32[2048,512]{1,0:T(8,128)} %own_ref, f32[1024,512]{1,0:T(8,128)} %collective-permute-done.8.recv_ref), custom_call_target="tpu_custom_call" | custom-call | tf_op jit(solution)/shard_map/turn_sigma/pallas_call | solution.py:122
  79.6 0.0 collective-permute-start.9
  79.7 15.0 %all-gather.3.cloned.1.call-done = f32[1280,2048]{1,0:T(8,128)} async-done(((f32[40,2048]{1,0:T(8,128)}), f32[1280,2048]{1,0:T(8,128)}) %all-gather.3.cloned.1.call-update) | async-done | bytes 10485776 | tf_op jit(solution)/shard_map/all_gather | solution.py:231
  94.6 1.6 copy-done.2
  96.2 1.6 copy-done.3
  97.8 12.2 %whole_products.1 = f32[32,40,512]{2,1,0:T(8,128)} custom-call(s32[32]{0:T(128)S(1)} %fusion.2.tab_ref, f32[32,40,2048]{2,1,0:T(8,128)} %bitcast.40, bf16[2048,512]{1,0:T(8,128)(2,1)S(1)} %copy-done.2, bf16[2048,512]{1,0:T(8,128)(2,1)S(1)} %copy-done.3), custom_call_target="tpu_custom_call" | custom-call | flops 8053063680 | bytes 18874368 | tf_op jit(solution)/shard_map/whole_products/pallas_call | solution.py:92
  110.1 1.0 copy-done.4
  111.1 1.6 copy-done
  112.7 1.6 copy-done.1
  114.3 1.4 copy-done.5
  115.7 5.8 %turned_products.1 = (f32[8,24,1024]{2,1,0:T(8,128)S(1)}, f32[8,24,1024]{2,1,0:T(8,128)S(1)}, f32[4,24,1024]{2,1,0:T(8,128)S(1)}, f32[4,24,1024]{2,1,0:T(8,128)S(1)}, f32[8,24,1024]{2,1,0:T(8,128)S(1)}) custom-call(s32[2,32]{1,0:T(2,128)S(1)} %pad_add_fusion.tab_ref, f32[32,24,512]{2,1,0:T(8,128)S(1)} %pad_maximum_fusion.own_ref, ...), custom_call_target="tpu_custom_call" | custom-call | flops 4831838208 | bytes 10485760 | tf_op jit(solution)/shard_map/turned_products/pallas_call | solution.py:162
  121.5 0.9 collective-permute-start.12
  122.4 1.4 collective-permute-start.10
  123.8 9.2 %collective-permute-done.12 = f32[4,24,1024]{2,1,0:T(8,128)S(1)} collective-permute-done((f32[4,24,1024]{2,1,0:T(8,128)S(1)}, f32[4,24,1024]{2,1,0:T(8,128)S(1)}, u32[]{:S(2)}, u32[]{:S(2)}) %collective-permute-start.12) | collective-permute-done | bytes 393248 | tf_op jit(solution)/shard_map/ppermute | solution.py:48
  133.0 0.1 fusion.28
  133.1 0.1 pad_maximum_fusion.2
  133.2 0.7 collective-permute-start.13
  133.9 0.1 slice_add_fusion.1
  134.0 0.1 pad_maximum_fusion.1
  134.0 1.5 collective-permute-start.11
  135.5 10.6 %reduce-scatter.2.cloned.1.call-done = f32[8,40,512]{2,1,0:T(8,128)} async-done(((f32[32,40,512]{2,1,0:T(8,128)}), f32[8,40,512]{2,1,0:T(8,128)}) %reduce-scatter.2.cloned.1.call-update) | async-done | bytes 655376 | tf_op jit(solution)/shard_map/reduce_scatter | solution.py:252
  146.1 1.1 slice.75
  147.2 4.9 %collective-permute-start.14 = (f32[4,40,512]{2,1,0:T(8,128)S(1)}, f32[4,40,512]{2,1,0:T(8,128)S(1)}, u32[]{:S(2)}, u32[]{:S(2)}) collective-permute-start(f32[4,40,512]{2,1,0:T(8,128)S(1)} %slice.75), channel_id=1, source_target_pairs={{0,128},{1,129},{2,130},{3,131},{4,132},{5,133},{6,134},{7,135},{8... | collective-permute-start | bytes 983048 | tf_op jit(solution)/shard_map/ppermute | solution.py:48
  152.2 0.6 copy.7
  152.8 0.1 collective-permute-done.11
  152.9 1.3 add_add_fusion
  154.2 13.5 %collective-permute-done.14 = f32[4,40,512]{2,1,0:T(8,128)S(1)} collective-permute-done((f32[4,40,512]{2,1,0:T(8,128)S(1)}, f32[4,40,512]{2,1,0:T(8,128)S(1)}, u32[]{:S(2)}, u32[]{:S(2)}) %collective-permute-start.14) | collective-permute-done | bytes 327712 | tf_op jit(solution)/shard_map/ppermute | solution.py:48
  167.9 1.6 collective-permute-start.19
  169.5 0.5 collective-permute-start.21
  170.0 1.1 collective-permute-start.20
  171.1 1.0 collective-permute-start.18
  172.0 3.1 %collective-permute-start.17 = (f32[40,512]{1,0:T(8,128)S(1)}, f32[40,512]{1,0:T(8,128)S(1)}, u32[]{:S(2)}, u32[]{:S(2)}) collective-permute-start(f32[40,512]{1,0:T(8,128)S(1)} %get-tuple-element.64), channel_id=1, source_target_pairs={{0,2},{1,3},{2,0},{3,1},{4,34},{5,35},{6,32},{7,33},{8,66},{9,67},... | collective-permute-start | bytes 245768 | tf_op jit(solution)/shard_map/ppermute | solution.py:48
  175.1 6.7 %collective-permute-done.19 = f32[2,24,1024]{2,1,0:T(8,128)S(1)} collective-permute-done((f32[2,24,1024]{2,1,0:T(8,128)S(1)}, f32[2,24,1024]{2,1,0:T(8,128)S(1)}, u32[]{:S(2)}, u32[]{:S(2)}) %collective-permute-start.19) | collective-permute-done | bytes 196640 | tf_op jit(solution)/shard_map/ppermute | solution.py:48
  181.8 8.0 %collective-permute-start.15 = (f32[40,512]{1,0:T(8,128)S(1)}, f32[40,512]{1,0:T(8,128)S(1)}, u32[]{:S(2)}, u32[]{:S(2)}) collective-permute-start(f32[40,512]{1,0:T(8,128)S(1)} %get-tuple-element.66), channel_id=1, source_target_pairs={{0,0},{1,1},{2,2},{3,3},{4,32},{5,33},{6,34},{7,35},{8,64},{9,65},... | collective-permute-start | bytes 245768 | tf_op jit(solution)/shard_map/ppermute | solution.py:48
  189.8 3.7 %collective-permute-done.20 = f32[2,24,1024]{2,1,0:T(8,128)S(1)} collective-permute-done((f32[2,24,1024]{2,1,0:T(8,128)S(1)}, f32[2,24,1024]{2,1,0:T(8,128)S(1)}, u32[]{:S(2)}, u32[]{:S(2)}) %collective-permute-start.20) | collective-permute-done | bytes 196640 | tf_op jit(solution)/shard_map/ppermute | solution.py:48
  193.5 0.1 add_add_fusion.1
  193.6 0.7 slice_bitcast_fusion
  194.3 0.6 pad_add_fusion.1.shift_ref
  194.9 0.7 collective-permute-done.22.refs_5_
  195.6 0.6 copy-done.8
  196.3 2.1 finish.1
  198.3 0.9 reduce_sum.18
  199.2 20.4 %all_to_all.6 = f32[8,1,64]{2,1,0:T(1,128)S(1)} all-to-all(f32[8,1,64]{2,1,0:T(1,128)S(1)} %broadcast_in_dim.14), channel_id=1, replica_groups=mesh['row'=8,'col'=32] {'row'}, dimensions={0} | all-to-all | bytes 4096 | tf_op jit(solution)/shard_map/all_to_all | solution.py:270
  219.6 0.5 add.435
  (58 shorter events, 0.5 us)
Async XLA Ops:
  7.2 87.5 %all-gather.3.cloned.1.call-start = ((), (), s32[]{:S(2)}) async-start(), calls=%async_computation.3 | async-start | bytes 10813440 | tf_op jit(solution)/shard_map/all_gather | solution.py:231
  9.2 43.5 %copy-start.6 = (f32[64,2048]{1,0:T(8,128)}, f32[64,2048]{1,0:T(8,128)S(1)}, u32[]{:S(2)}) copy-start(f32[64,2048]{1,0:T(8,128)S(1)} %broadcast_multiply_fusion.masked_ref) | copy-start | bytes 1572868
  10.0 136.1 %reduce-scatter.2.cloned.1.call-start = ((), (), s32[]{:S(2)}) async-start(), calls=%async_computation.2 | async-start | bytes 3276800 | tf_op jit(solution)/shard_map/reduce_scatter | solution.py:252
  10.2 13.7 %collective-permute-start.3 = (f32[24,512]{1,0:T(8,128)S(1)}, f32[24,512]{1,0:T(8,128)S(1)}, u32[]{:S(2)}, u32[]{:S(2)}) collective-permute-start(f32[24,512]{1,0:T(8,128)S(1)} %get-tuple-element.69), channel_id=1, source_target_pairs={{0,3},{1,0},{2,1},{3,2},{4,35},{5,32},{6,33},{7,34},{8,67},{9,64},... | collective-permute-start | bytes 147464 | tf_op jit(solution)/shard_map/ppermute | solution.py:48
  12.2 11.6 %collective-permute-start.2 = (f32[24,512]{1,0:T(8,128)S(1)}, f32[24,512]{1,0:T(8,128)S(1)}, u32[]{:S(2)}, u32[]{:S(2)}) collective-permute-start(f32[24,512]{1,0:T(8,128)S(1)} %get-tuple-element.70), channel_id=1, source_target_pairs={{0,2},{1,3},{2,0},{3,1},{4,34},{5,35},{6,32},{7,33},{8,66},{9,67},... | collective-permute-start | bytes 147464 | tf_op jit(solution)/shard_map/ppermute | solution.py:48
  14.7 9.1 %collective-permute-start.1 = (f32[24,512]{1,0:T(8,128)S(1)}, f32[24,512]{1,0:T(8,128)S(1)}, u32[]{:S(2)}, u32[]{:S(2)}) collective-permute-start(f32[24,512]{1,0:T(8,128)S(1)} %get-tuple-element.71), channel_id=1, source_target_pairs={{0,1},{1,2},{2,3},{3,0},{4,33},{5,34},{6,35},{7,32},{8,65},{9,66},... | collective-permute-start | bytes 147464 | tf_op jit(solution)/shard_map/ppermute | solution.py:48
  19.4 11.4 %collective-permute-start = (f32[24,512]{1,0:T(8,128)S(1)}, f32[24,512]{1,0:T(8,128)S(1)}, u32[]{:S(2)}, u32[]{:S(2)}) collective-permute-start(f32[24,512]{1,0:T(8,128)S(1)} %get-tuple-element.72), channel_id=1, source_target_pairs={{0,0},{1,1},{2,2},{3,3},{4,32},{5,33},{6,34},{7,35},{8,64},{9,65},... | collective-permute-start | bytes 147464 | tf_op jit(solution)/shard_map/ppermute | solution.py:48
  30.8 18.7 %collective-permute-start.4 = (f32[4,24,512]{2,1,0:T(8,128)S(1)}, f32[4,24,512]{2,1,0:T(8,128)S(1)}, u32[]{:S(2)}, u32[]{:S(2)}) collective-permute-start(f32[4,24,512]{2,1,0:T(8,128)S(1)} %pad_maximum_fusion.3), channel_id=1, source_target_pairs={{0,128},{1,129},{2,130},{3,131},{4,132},{5,133},{6,134},{7,135},{8... | collective-permute-start | bytes 589832 | tf_op jit(solution)/shard_map/ppermute | solution.py:48
  52.7 21.6 %collective-permute-start.8 = (f32[1024,512]{1,0:T(8,128)}, f32[1024,512]{1,0:T(8,128)}, u32[]{:S(2)}, u32[]{:S(2)}) collective-permute-start(f32[1024,512]{1,0:T(8,128)} %constant_dynamic-slice_fusion), channel_id=1, source_target_pairs={{0,1},{1,0},{2,3},{3,2},{4,5},{5,4},{6,7},{7,6},{8,9},{9,8},{10,11... | collective-permute-start | bytes 6291464 | tf_op jit(solution)/shard_map/ppermute | solution.py:48
  52.7 11.9 %collective-permute-start.7 = (f32[8,24,512]{2,1,0:T(8,128)S(1)}, f32[8,24,512]{2,1,0:T(8,128)S(1)}, u32[]{:S(2)}, u32[]{:S(2)}) collective-permute-start(f32[8,24,512]{2,1,0:T(8,128)S(1)} %constant_dynamic-update-slice_fusion), channel_id=1, source_target_pairs={{0,96},{1,97},{2,98},{3,99},{4,100},{5,101},{6,102},{7,103},{8,104... | collective-permute-start | bytes 1179656 | tf_op jit(solution)/shard_map/ppermute | solution.py:48
  52.7 13.6 %collective-permute-start.6 = (f32[8,24,512]{2,1,0:T(8,128)S(1)}, f32[8,24,512]{2,1,0:T(8,128)S(1)}, u32[]{:S(2)}, u32[]{:S(2)}) collective-permute-start(f32[8,24,512]{2,1,0:T(8,128)S(1)} %constant_dynamic-update-slice_fusion), channel_id=1, source_target_pairs={{0,64},{1,65},{2,66},{3,67},{4,68},{5,69},{6,70},{7,71},{8,72},{9,... | collective-permute-start | bytes 1179656 | tf_op jit(solution)/shard_map/ppermute | solution.py:48
  52.8 21.4 %collective-permute-start.5 = (f32[8,24,512]{2,1,0:T(8,128)S(1)}, f32[8,24,512]{2,1,0:T(8,128)S(1)}, u32[]{:S(2)}, u32[]{:S(2)}) collective-permute-start(f32[8,24,512]{2,1,0:T(8,128)S(1)} %constant_dynamic-update-slice_fusion), channel_id=1, source_target_pairs={{0,32},{1,33},{2,34},{3,35},{4,36},{5,37},{6,38},{7,39},{8,40},{9,... | collective-permute-start | bytes 1179656 | tf_op jit(solution)/shard_map/ppermute | solution.py:48
  79.6 30.4 %collective-permute-start.9 = (f32[32,24,512]{2,1,0:T(8,128)S(1)}, f32[32,24,512]{2,1,0:T(8,128)S(1)}, u32[]{:S(2)}, u32[]{:S(2)}) collective-permute-start(f32[32,24,512]{2,1,0:T(8,128)S(1)} %pad_maximum_fusion.own_ref), channel_id=1, source_target_pairs={{0,1},{1,0},{2,3},{3,2},{4,5},{5,4},{6,7},{7,6},{8,9},{9,8},{10,11... | collective-permute-start | bytes 4718600 | tf_op jit(solution)/shard_map/ppermute | solution.py:48
  94.6 1.6 copy-start.2
  96.2 1.6 copy-start.3
  110.0 1.1 copy-start.4
  111.1 1.6 copy-start
  112.7 1.6 copy-start.1
  114.3 1.4 copy-start.5
  121.5 11.5 %collective-permute-start.12 = (f32[4,24,1024]{2,1,0:T(8,128)S(1)}, f32[4,24,1024]{2,1,0:T(8,128)S(1)}, u32[]{:S(2)}, u32[]{:S(2)}) collective-permute-start(f32[4,24,1024]{2,1,0:T(8,128)S(1)} %get-tuple-element.45), channel_id=1, source_target_pairs={{0,6},{1,7},{2,0},{3,1},{4,2},{5,3},{6,4},{7,5},{8,14},{9,15},{10,... | collective-permute-start | bytes 1179656 | tf_op jit(solution)/shard_map/ppermute | solution.py:48
  122.4 11.5 %collective-permute-start.10 = (f32[4,24,1024]{2,1,0:T(8,128)S(1)}, f32[4,24,1024]{2,1,0:T(8,128)S(1)}, u32[]{:S(2)}, u32[]{:S(2)}) collective-permute-start(f32[4,24,1024]{2,1,0:T(8,128)S(1)} %get-tuple-element.43), channel_id=1, source_target_pairs={{0,2},{1,3},{2,4},{3,5},{4,6},{5,7},{6,0},{7,1},{8,10},{9,11},{10,... | collective-permute-start | bytes 1179656 | tf_op jit(solution)/shard_map/ppermute | solution.py:48
  133.2 19.6 %collective-permute-start.13 = (f32[8,24,1024]{2,1,0:T(8,128)S(1)}, f32[8,24,1024]{2,1,0:T(8,128)S(1)}, u32[]{:S(2)}, u32[]{:S(2)}) collective-permute-start(f32[8,24,1024]{2,1,0:T(8,128)S(1)} %pad_maximum_fusion.2), channel_id=1, source_target_pairs={{0,6},{1,7},{2,0},{3,1},{4,2},{5,3},{6,4},{7,5},{8,14},{9,15},{10,... | collective-permute-start | bytes 2359304 | tf_op jit(solution)/shard_map/ppermute | solution.py:48
  134.0 18.9 %collective-permute-start.11 = (f32[8,24,1024]{2,1,0:T(8,128)S(1)}, f32[8,24,1024]{2,1,0:T(8,128)}, u32[]{:S(2)}, u32[]{:S(2)}) collective-permute-start(f32[8,24,1024]{2,1,0:T(8,128)S(1)} %pad_maximum_fusion.1), channel_id=1, source_target_pairs={{0,2},{1,3},{2,4},{3,5},{4,6},{5,7},{6,0},{7,1},{8,10},{9,11},{10,... | collective-permute-start | bytes 2359304 | tf_op jit(solution)/shard_map/ppermute | solution.py:48
  146.1 21.6 %copy-start.7 = (f32[8,40,512]{2,1,0:T(8,128)S(1)}, f32[8,40,512]{2,1,0:T(8,128)}, u32[]{:S(2)}) copy-start(f32[8,40,512]{2,1,0:T(8,128)} %reduce-scatter.2.cloned.1.call-done) | copy-start | bytes 1966084
  147.2 20.5 %collective-permute-start.14 = (f32[4,40,512]{2,1,0:T(8,128)S(1)}, f32[4,40,512]{2,1,0:T(8,128)S(1)}, u32[]{:S(2)}, u32[]{:S(2)}) collective-permute-start(f32[4,40,512]{2,1,0:T(8,128)S(1)} %slice.75), channel_id=1, source_target_pairs={{0,128},{1,129},{2,130},{3,131},{4,132},{5,133},{6,134},{7,135},{8... | collective-permute-start | bytes 983048 | tf_op jit(solution)/shard_map/ppermute | solution.py:48
  167.8 51.9 %copy-start.13 = (f32[64]{0:T(128)S(1)}, f32[64]{0:T(128)}, u32[]{:S(2)}) copy-start(f32[64]{0:T(128)} %param.7) | copy-start | bytes 772
  167.9 14.0 %collective-permute-start.19 = (f32[2,24,1024]{2,1,0:T(8,128)S(1)}, f32[2,24,1024]{2,1,0:T(8,128)S(1)}, u32[]{:S(2)}, u32[]{:S(2)}) collective-permute-start(f32[2,24,1024]{2,1,0:T(8,128)S(1)} %get-tuple-element.56), channel_id=1, source_target_pairs={{0,8},{1,9},{2,10},{3,11},{4,12},{5,13},{6,14},{7,15},{8,16},{9,17... | collective-permute-start | bytes 589832 | tf_op jit(solution)/shard_map/ppermute | solution.py:48
  169.5 12.3 %collective-permute-start.21 = (f32[2,24,1024]{2,1,0:T(8,128)S(1)}, f32[2,24,1024]{2,1,0:T(8,128)S(1)}, u32[]{:S(2)}, u32[]{:S(2)}) collective-permute-start(f32[2,24,1024]{2,1,0:T(8,128)S(1)} %get-tuple-element.57), channel_id=1, source_target_pairs={{0,24},{1,25},{2,26},{3,27},{4,28},{5,29},{6,30},{7,31},{8,0},{9,1... | collective-permute-start | bytes 589832 | tf_op jit(solution)/shard_map/ppermute | solution.py:48
  170.0 23.5 %collective-permute-start.20 = (f32[2,24,1024]{2,1,0:T(8,128)S(1)}, f32[2,24,1024]{2,1,0:T(8,128)S(1)}, u32[]{:S(2)}, u32[]{:S(2)}) collective-permute-start(f32[2,24,1024]{2,1,0:T(8,128)S(1)} %get-tuple-element.58), channel_id=1, source_target_pairs={{0,16},{1,17},{2,18},{3,19},{4,20},{5,21},{6,22},{7,23},{8,24},{9,... | collective-permute-start | bytes 589832 | tf_op jit(solution)/shard_map/ppermute | solution.py:48
  171.1 22.5 %collective-permute-start.18 = (f32[40,512]{1,0:T(8,128)S(1)}, f32[40,512]{1,0:T(8,128)S(1)}, u32[]{:S(2)}, u32[]{:S(2)}) collective-permute-start(f32[40,512]{1,0:T(8,128)S(1)} %get-tuple-element.63), channel_id=1, source_target_pairs={{0,3},{1,0},{2,1},{3,2},{4,35},{5,32},{6,33},{7,34},{8,67},{9,64},... | collective-permute-start | bytes 245768 | tf_op jit(solution)/shard_map/ppermute | solution.py:48
  172.0 21.5 %collective-permute-start.17 = (f32[40,512]{1,0:T(8,128)S(1)}, f32[40,512]{1,0:T(8,128)S(1)}, u32[]{:S(2)}, u32[]{:S(2)}) collective-permute-start(f32[40,512]{1,0:T(8,128)S(1)} %get-tuple-element.64), channel_id=1, source_target_pairs={{0,2},{1,3},{2,0},{3,1},{4,34},{5,35},{6,32},{7,33},{8,66},{9,67},... | collective-permute-start | bytes 245768 | tf_op jit(solution)/shard_map/ppermute | solution.py:48
  181.8 11.8 %collective-permute-start.16 = (f32[40,512]{1,0:T(8,128)S(1)}, f32[40,512]{1,0:T(8,128)S(1)}, u32[]{:S(2)}, u32[]{:S(2)}) collective-permute-start(f32[40,512]{1,0:T(8,128)S(1)} %get-tuple-element.65), channel_id=1, source_target_pairs={{0,1},{1,2},{2,3},{3,0},{4,33},{5,34},{6,35},{7,32},{8,65},{9,66},... | collective-permute-start | bytes 245768 | tf_op jit(solution)/shard_map/ppermute | solution.py:48
  181.8 11.8 %collective-permute-start.15 = (f32[40,512]{1,0:T(8,128)S(1)}, f32[40,512]{1,0:T(8,128)S(1)}, u32[]{:S(2)}, u32[]{:S(2)}) collective-permute-start(f32[40,512]{1,0:T(8,128)S(1)} %get-tuple-element.66), channel_id=1, source_target_pairs={{0,0},{1,1},{2,2},{3,3},{4,32},{5,33},{6,34},{7,35},{8,64},{9,65},... | collective-permute-start | bytes 245768 | tf_op jit(solution)/shard_map/ppermute | solution.py:48
  193.5 2.1 copy-start.9
  193.6 2.1 copy-start.10
  193.6 2.1 copy-start.11
  193.6 2.0 copy-start.12
  194.3 1.3 collective-permute-start.22
  195.6 0.6 copy-start.8
Sparse Core Ops, SparseCore 0:
  10.4 84.1 all-gather.2
  110.1 35.9 reduce-scatter.1

commit v2 on v1

--- a/solution.py
+++ b/solution.py
@@ -77,9 +77,11 @@
     step = pl.program_id(0)
     blocks, rows, depth = rows_ref.shape
     hi, lo = split(rows_ref[...].reshape(blocks * rows, depth))
+    both, count = jnp.concatenate([hi, lo]), hi.shape[0]
     for n in range(0, out_ref.shape[2], 256):
         dot = lambda a, b: jnp.dot(a, b[:, n : n + 256], preferred_element_type=F32)
-        acc = dot(lo, sh_ref) + dot(hi, sl_ref) + dot(hi, sh_ref)
+        acc = dot(both, sh_ref)
+        acc = acc[:count] + acc[count:] + dot(hi, sl_ref)
         for b in range(blocks):
             out_ref[tab_ref[step * blocks + b], :, n : n + 256] = acc[b * rows : (b + 1) * rows]
 
@@ -100,7 +102,7 @@
         ],
         out_specs=pl.BlockSpec((blocks, rows, width), lambda i: (0, 0, 0)),
         out_shape=jax.ShapeDtypeStruct((blocks, rows, width), F32),
-        compiler_params=pltpu.CompilerParams(vmem_limit_bytes=40 * 2**20),
+        compiler_params=pltpu.CompilerParams(vmem_limit_bytes=60 * 2**20),
         cost_estimate=pl.CostEstimate(
             flops=6 * blocks * rows * depth * width,
             bytes_accessed=blocks * rows * depth * 4 + 2**23,
@@ -143,10 +145,12 @@
             at = pl.ds(pl.multiple_of(tab_ref[side, b] * rows, rows), rows)
             rows_ref[at, side * n : side * n + n] = ref[b]
     hi, lo = split(rows_ref[...])
+    both, count = jnp.concatenate([hi, lo]), hi.shape[0]
     for c in range(0, sh_ref.shape[1], 256):
         columns = slice(c, c + 256)
         dot = lambda a, b: jnp.dot(a, b[:, columns], preferred_element_type=F32)
-        acc = dot(lo, sh_ref) + dot(hi, sl_ref) + dot(hi, sh_ref)
+        acc = dot(both, sh_ref)
+        acc = acc[:count] + acc[count:] + dot(hi, sl_ref)
         at = 0
         for out in outs:
             for b in range(out.shape[0]):
@@ -165,7 +169,7 @@
         out_specs=[vmem] * 5,
         out_shape=[jax.ShapeDtypeStruct((n, rows, width), F32) for n in (8, 8, 4, 4, 8)],
         scratch_shapes=[pltpu.VMEM((total, 2 * n), F32)],
-        compiler_params=pltpu.CompilerParams(vmem_limit_bytes=40 * 2**20),
+        compiler_params=pltpu.CompilerParams(vmem_limit_bytes=60 * 2**20),
         cost_estimate=pl.CostEstimate(
             flops=6 * total * 2 * n * width, bytes_accessed=total * 8192 + 2**22, transcendentals=0
         ),
@@ -175,7 +179,7 @@
 
 def final_kernel(shift_ref, mask_ref, masked_ref, *refs):
     blocks, halves, (off_ref, var_ref) = refs[:4], refs[4:6], refs[6:]
-    at = 0
+    at, sums = 0, []
     for pieces, places, width in ((blocks, (0, 1, 2, 3), 512), (halves, (4, 5), 1024)):
         rows = pieces[0].shape[0]
         total = jnp.zeros((rows, 128), F32)
@@ -186,8 +190,16 @@
             part = product * masked_ref[at : at + rows, columns]
             for n in range(0, width, 128):
                 total += part[:, n : n + 128]
-        var_ref[at : at + rows, :] = total
+        sums.append(total)
         at += rows
+    sums = jnp.concatenate(sums)
+    var_ref[...] = lax.dot_general(
+        jnp.ones((8, 128), F32),
+        sums,
+        (((1,), (1,)), ((), ())),
+        precision=lax.Precision.HIGHEST,
+        preferred_element_type=F32,
+    )
 
 
 def finish(shift, mask, masked, groups):
@@ -198,7 +210,7 @@
         out_specs=[vmem] * 2,
         out_shape=[
             jax.ShapeDtypeStruct(masked.shape, F32),
-            jax.ShapeDtypeStruct((masked.shape[0], 128), F32),
+            jax.ShapeDtypeStruct((8, masked.shape[0]), F32),
         ],
         name="finish",
     )(shift, mask, masked, *groups)
@@ -255,7 +267,6 @@
     left = jnp.concatenate([left[:4], left[4:] + send(far_left, along_x(-1))])
     here = here + send(right, along_x(1)) + send(left, along_x(-1))
     first = sum_zh(first)
-    here, first = tie(here, first)
     groups = [send(first[n], regroup(n)) for n in range(4)]
     total = here[:2]
     for n in (1, 2, 3):
@@ -264,9 +275,7 @@
     groups += [total[0], send(total[1], OTHER_CORE)]
 
     shift = jnp.concatenate([(col - jnp.arange(4, dtype=jnp.int32)) % 4, jnp.stack([core, 1 - core])])
-    sigma_off, var_lanes = finish(shift, mask, masked, groups)
-    part = jnp.sum(var_lanes, axis=1)
-    shares = jnp.broadcast_to(part[None, :], (8, part.shape[0]))
+    sigma_off, shares = finish(shift, mask, masked, groups)
     shares = lax.all_to_all(shares, "row", 0, 0, tiled=True)
     return sigma_off, base_var + jnp.sum(shares, axis=0)
 

time: 232 us -> 225 us (0.970)
  local copies, waits for them, and re-layouts: 16.1 us -> 8.81 us
  Pallas kernels: 32.1 us -> 37.7 us
  other arithmetic: 5.7 us -> 9.59 us
  waiting for transfers between devices: 85.3 us -> 81.7 us
    unnamed x35 -> x31, local copies, waits for them, and re-layouts: 10.2 us -> 3.03 us
    all_gather x1, waiting for transfers between devices: 15 us -> 10.5 us  [body(): gathered = lax.all_gather(masked[:FIRST], 'col')]
    pallas_call x1, Pallas kernels: 5.8 us -> 9.91 us  [turned_products(): pl.pallas_call(turned_kernel, in_specs=[pl.BlockSpec(memory_space=pltpu.S...]
  transfers between devices with their start and end apart: 25 -> 25, of which waited for: 13 -> 14; matrix products, arithmetic and copies ran while one was open for 3% -> 5% of each run, Pallas kernels for 13% -> 16%
where the time goes in v2:
time: 225 us; the launch traced here: 222 us
  waiting for transfers between devices  81.7 us (36%)
  starting transfers between devices  51.4 us (23%)
  Pallas kernels  37.7 us (17%)
  blocking collectives  18.5 us (8%)
  between operations  14.5 us (6%)
  other arithmetic  9.59 us (4%)
  local copies, waits for them, and re-layouts  8.81 us (4%)
    ppermute x23, waiting for transfers between devices, send(): return lax.ppermute(value, AXES, perm)  61.6 us
    ppermute x23, starting transfers between devices, send(): return lax.ppermute(value, AXES, perm)  51.3 us
    all_to_all x1, blocking collectives, body(): shares = lax.all_to_all(shares, 'row', 0, 0, tiled=True)  18.5 us
    pallas_call x1, Pallas kernels, whole_products(): pl.pallas_call(whole_kernel, grid=(blocks // group,), in_specs=[pl.BlockS...  13.6 us
    all_gather x1, waiting for transfers between devices, body(): gathered = lax.all_gather(masked[:FIRST], 'col')  10.5 us
    pallas_call x1, Pallas kernels, turned_products(): pl.pallas_call(turned_kernel, in_specs=[pl.BlockSpec(memory_space=pltpu.S...  9.91 us
    reduce_scatter x1, waiting for transfers between devices, body(): lax.psum_scatter(first, 'row', scatter_dimension=0, axis_index_groups=pai...  9.54 us
    pallas_call x1, Pallas kernels, split_all(): pl.pallas_call(split_kernel, grid=(value.shape[0] // 256,), in_specs=[spe...  6.81 us
  transfers between devices with their start and end apart: 25, of which 14 were waited for; matrix products, arithmetic and copies ran while one was open for 5% of the time, Pallas kernels for 16%

profile of v2, /device:TPU:36, one launch (start us, length us, event | category | flops | bytes accessed | tf_op | source)
XLA Modules:
  0.0 222.2 jit_solution(1675423823746328868)
XLA Ops:
  7.2 0.0 all-gather.3.cloned.1.call-start
  7.2 0.8 convert_bitcast_fusion
  8.0 0.1 broadcast_bitcast_fusion
  8.1 1.1 broadcast_multiply_fusion.masked_ref
  9.2 0.8 slice.72
  10.0 0.0 reduce-scatter.2.cloned.1.call-start
  10.2 2.0 collective-permute-start.3
  12.2 2.5 %collective-permute-start.2 = (f32[24,512]{1,0:T(8,128)S(1)}, f32[24,512]{1,0:T(8,128)S(1)}, u32[]{:S(2)}, u32[]{:S(2)}) collective-permute-start(f32[24,512]{1,0:T(8,128)S(1)} %get-tuple-element.66), channel_id=1, source_target_pairs={{0,2},{1,3},{2,0},{3,1},{4,34},{5,35},{6,32},{7,33},{8,66},{9,67},... | collective-permute-start | bytes 147464 | tf_op jit(solution)/shard_map/ppermute | solution.py:48
  14.7 4.6 %collective-permute-start.1 = (f32[24,512]{1,0:T(8,128)S(1)}, f32[24,512]{1,0:T(8,128)S(1)}, u32[]{:S(2)}, u32[]{:S(2)}) collective-permute-start(f32[24,512]{1,0:T(8,128)S(1)} %get-tuple-element.67), channel_id=1, source_target_pairs={{0,1},{1,2},{2,3},{3,0},{4,33},{5,34},{6,35},{7,32},{8,65},{9,66},... | collective-permute-start | bytes 147464 | tf_op jit(solution)/shard_map/ppermute | solution.py:48
  19.4 4.4 %collective-permute-start = (f32[24,512]{1,0:T(8,128)S(1)}, f32[24,512]{1,0:T(8,128)S(1)}, u32[]{:S(2)}, u32[]{:S(2)}) collective-permute-start(f32[24,512]{1,0:T(8,128)S(1)} %get-tuple-element.68), channel_id=1, source_target_pairs={{0,0},{1,1},{2,2},{3,3},{4,32},{5,33},{6,34},{7,35},{8,64},{9,65},... | collective-permute-start | bytes 147464 | tf_op jit(solution)/shard_map/ppermute | solution.py:48
  23.9 6.9 %collective-permute-done = f32[24,512]{1,0:T(8,128)S(1)} collective-permute-done((f32[24,512]{1,0:T(8,128)S(1)}, f32[24,512]{1,0:T(8,128)S(1)}, u32[]{:S(2)}, u32[]{:S(2)}) %collective-permute-start) | collective-permute-done | bytes 49184 | tf_op jit(solution)/shard_map/ppermute | solution.py:48
  30.8 12.5 %collective-permute-start.4 = (f32[4,24,512]{2,1,0:T(8,128)S(1)}, f32[4,24,512]{2,1,0:T(8,128)S(1)}, u32[]{:S(2)}, u32[]{:S(2)}) collective-permute-start(f32[4,24,512]{2,1,0:T(8,128)S(1)} %pad_maximum_fusion.3), channel_id=1, source_target_pairs={{0,128},{1,129},{2,130},{3,131},{4,132},{5,133},{6,134},{7,135},{8... | collective-permute-start | bytes 589832 | tf_op jit(solution)/shard_map/ppermute | solution.py:48
  43.3 6.1 %collective-permute-done.4 = f32[4,24,512]{2,1,0:T(8,128)S(1)} collective-permute-done((f32[4,24,512]{2,1,0:T(8,128)S(1)}, f32[4,24,512]{2,1,0:T(8,128)S(1)}, u32[]{:S(2)}, u32[]{:S(2)}) %collective-permute-start.4) | collective-permute-done | bytes 196640 | tf_op jit(solution)/shard_map/ppermute | solution.py:48
  49.5 3.2 %constant_dynamic-slice_fusion = f32[1024,512]{1,0:T(8,128)} fusion(f32[2048,512]{1,0:T(8,128)} %own_ref, s32[]{:T(128)S(6)} %select_n.326), kind=kLoop, calls=%fused_computation.65 | loop fusion | bytes 4194308 | tf_op jit(solution)/shard_map/dynamic_slice | solution.py:254
  52.6 0.1 collective-permute-start.6
  52.7 1.9 collective-permute-start.5
  54.7 6.8 %split_sigma.1 = (bf16[2048,512]{1,0:T(8,128)(2,1)}, bf16[2048,512]{1,0:T(8,128)(2,1)}) custom-call(f32[2048,512]{1,0:T(8,128)} %own_ref), custom_call_target="tpu_custom_call" | custom-call | tf_op jit(solution)/shard_map/split_sigma/pallas_call | solution.py:66
  61.5 3.1 %collective-permute-done.7 = f32[8,24,512]{2,1,0:T(8,128)S(1)} collective-permute-done((f32[8,24,512]{2,1,0:T(8,128)S(1)}, f32[8,24,512]{2,1,0:T(8,128)S(1)}, u32[]{:S(2)}, u32[]{:S(2)}) %collective-permute-start.7) | collective-permute-done | bytes 393248 | tf_op jit(solution)/shard_map/ppermute | solution.py:48
  64.5 1.7 collective-permute-done.6
  66.2 8.0 %collective-permute-done.5 = f32[8,24,512]{2,1,0:T(8,128)} collective-permute-done((f32[8,24,512]{2,1,0:T(8,128)S(1)}, f32[8,24,512]{2,1,0:T(8,128)}, u32[]{:S(2)}, u32[]{:S(2)}) %collective-permute-start.5) | collective-permute-done | bytes 393248 | tf_op jit(solution)/shard_map/ppermute | solution.py:48
  74.2 2.3 %pad_maximum_fusion.own_ref = f32[32,24,512]{2,1,0:T(8,128)} fusion(f32[8,24,512]{2,1,0:T(8,128)S(1)} %collective-permute-done.7, f32[8,24,512]{2,1,0:T(8,128)S(1)} %collective-permute-done.6, f32[8,24,512]{2,1,0:T(8,128)} %collective-permute-done.5, f32[8,24,512]{2,1,0:T(8,128)S(1)} %constant_dynamic-update-slice_fusion), kind=kLoop, calls=%fused_computation | loop fusion | flops 1179648 | bytes 3145728 | tf_op jit(solution)/shard_map/concatenate | solution.py:253
  76.5 1.4 copy-done.1
  77.9 5.3 %turn_sigma.1 = (bf16[1024,1024]{1,0:T(8,128)(2,1)}, bf16[1024,1024]{1,0:T(8,128)(2,1)}) custom-call(s32[1]{0:T(128)} %bitcast.core_ref, f32[2048,512]{1,0:T(8,128)} %own_ref, f32[1024,512]{1,0:T(8,128)} %copy-done.1), custom_call_target="tpu_custom_call" | custom-call | tf_op jit(solution)/shard_map/turn_sigma/pallas_call | solution.py:124
  83.2 0.0 collective-permute-start.9
  83.3 0.6 fusion.3.tab_ref
  83.8 10.5 %all-gather.3.cloned.1.call-done = f32[1280,2048]{1,0:T(8,128)} async-done(((f32[40,2048]{1,0:T(8,128)}), f32[1280,2048]{1,0:T(8,128)}) %all-gather.3.cloned.1.call-update) | async-done | bytes 10485776 | tf_op jit(solution)/shard_map/all_gather | solution.py:243
  94.4 13.6 %whole_products.1 = f32[32,40,512]{2,1,0:T(8,128)} custom-call(s32[32]{0:T(128)} %fusion.3.tab_ref, f32[32,40,2048]{2,1,0:T(8,128)} %bitcast.42, bf16[2048,512]{1,0:T(8,128)(2,1)} %get-tuple-element.33.sh_ref, bf16[2048,512]{1,0:T(8,128)(2,1)} %get-tuple-element.34.sl_ref), custom_call_target="tpu_custom_call" | custom-call | flops 8053063680 | bytes 18874368 | tf_op jit(solution)/shard_map/whole_products/pallas_call | solution.py:94
  108.1 0.8 pad_add_fusion.tab_ref
  108.8 0.3 copy-done.10
  109.1 9.9 %turned_products.1 = (f32[8,24,1024]{2,1,0:T(8,128)}, f32[8,24,1024]{2,1,0:T(8,128)}, f32[4,24,1024]{2,1,0:T(8,128)}, f32[4,24,1024]{2,1,0:T(8,128)}, f32[8,24,1024]{2,1,0:T(8,128)}) custom-call(s32[2,32]{1,0:T(2,128)} %pad_add_fusion.tab_ref, f32[32,24,512]{2,1,0:T(8,128)} %pad_maximum_fusion.own_ref, f32[32,24,512]{2,1,0:T(8,128)} %copy-done.10, ...), custom_call_target="tpu_custom_call" | custom-call | flops 4831838208 | bytes 10485760 | tf_op jit(solution)/shard_map/turned_products/pallas_call | solution.py:166
  119.0 0.8 collective-permute-start.17
  119.8 1.2 collective-permute-start.15
  121.0 9.4 %collective-permute-done.17 = f32[4,24,1024]{2,1,0:T(8,128)S(1)} collective-permute-done((f32[4,24,1024]{2,1,0:T(8,128)}, f32[4,24,1024]{2,1,0:T(8,128)S(1)}, u32[]{:S(2)}, u32[]{:S(2)}) %collective-permute-start.17) | collective-permute-done | bytes 393248 | tf_op jit(solution)/shard_map/ppermute | solution.py:48
  130.5 1.2 fusion.30
  131.7 0.1 pad_maximum_fusion.2
  131.8 0.9 collective-permute-start.18
  132.6 0.1 slice_add_fusion.1
  132.7 0.1 pad_maximum_fusion.1
  132.8 1.4 collective-permute-start.16
  134.2 0.6 copy.7
  134.8 9.5 %reduce-scatter.2.cloned.1.call-done = f32[8,40,512]{2,1,0:T(8,128)} async-done(((f32[32,40,512]{2,1,0:T(8,128)}), f32[8,40,512]{2,1,0:T(8,128)}) %reduce-scatter.2.cloned.1.call-update) | async-done | bytes 655376 | tf_op jit(solution)/shard_map/reduce_scatter | solution.py:264
  144.4 1.0 slice.75
  145.4 4.9 %collective-permute-start.10 = (f32[4,40,512]{2,1,0:T(8,128)S(1)}, f32[4,40,512]{2,1,0:T(8,128)S(1)}, u32[]{:S(2)}, u32[]{:S(2)}) collective-permute-start(f32[4,40,512]{2,1,0:T(8,128)S(1)} %slice.75), channel_id=1, source_target_pairs={{0,128},{1,129},{2,130},{3,131},{4,132},{5,133},{6,134},{7,135},{8... | collective-permute-start | bytes 983048 | tf_op jit(solution)/shard_map/ppermute | solution.py:48
  150.3 0.9 collective-permute-done.18
  151.2 0.5 collective-permute-done.16
  151.7 1.4 add_add_fusion
  153.1 1.2 collective-permute-start.19
  154.3 0.9 collective-permute-start.21
  155.2 1.6 collective-permute-start.20
  156.8 11.0 %collective-permute-done.10 = f32[4,40,512]{2,1,0:T(8,128)S(1)} collective-permute-done((f32[4,40,512]{2,1,0:T(8,128)S(1)}, f32[4,40,512]{2,1,0:T(8,128)S(1)}, u32[]{:S(2)}, u32[]{:S(2)}) %collective-permute-start.10) | collective-permute-done | bytes 327712 | tf_op jit(solution)/shard_map/ppermute | solution.py:48
  167.8 0.1 collective-permute-start.14
  167.9 0.1 collective-permute-start.13
  168.0 3.5 %collective-permute-done.19 = f32[2,24,1024]{2,1,0:T(8,128)S(1)} collective-permute-done((f32[2,24,1024]{2,1,0:T(8,128)S(1)}, f32[2,24,1024]{2,1,0:T(8,128)S(1)}, u32[]{:S(2)}, u32[]{:S(2)}) %collective-permute-start.19) | collective-permute-done | bytes 196640 | tf_op jit(solution)/shard_map/ppermute | solution.py:48
  171.5 2.7 %collective-permute-start.12 = (f32[40,512]{1,0:T(8,128)S(1)}, f32[40,512]{1,0:T(8,128)S(1)}, u32[]{:S(2)}, u32[]{:S(2)}) collective-permute-start(f32[40,512]{1,0:T(8,128)S(1)} %get-tuple-element.61), channel_id=1, source_target_pairs={{0,1},{1,2},{2,3},{3,0},{4,33},{5,34},{6,35},{7,32},{8,65},{9,66},... | collective-permute-start | bytes 245768 | tf_op jit(solution)/shard_map/ppermute | solution.py:48
  174.2 7.3 %collective-permute-start.11 = (f32[40,512]{1,0:T(8,128)S(1)}, f32[40,512]{1,0:T(8,128)S(1)}, u32[]{:S(2)}, u32[]{:S(2)}) collective-permute-start(f32[40,512]{1,0:T(8,128)S(1)} %get-tuple-element.62), channel_id=1, source_target_pairs={{0,0},{1,1},{2,2},{3,3},{4,32},{5,33},{6,34},{7,35},{8,64},{9,65},... | collective-permute-start | bytes 245768 | tf_op jit(solution)/shard_map/ppermute | solution.py:48
  181.5 9.9 %collective-permute-done.20 = f32[2,24,1024]{2,1,0:T(8,128)S(1)} collective-permute-done((f32[2,24,1024]{2,1,0:T(8,128)S(1)}, f32[2,24,1024]{2,1,0:T(8,128)S(1)}, u32[]{:S(2)}, u32[]{:S(2)}) %collective-permute-start.20) | collective-permute-done | bytes 196640 | tf_op jit(solution)/shard_map/ppermute | solution.py:48
  191.5 0.1 fusion.1
  191.6 0.7 slice_bitcast_fusion
  192.3 0.6 pad_add_fusion.1.shift_ref
  192.9 0.7 collective-permute-done.22.refs_5_
  193.6 0.6 copy-done.5
  194.2 2.1 finish.1
  196.3 18.5 %all_to_all.9 = f32[8,1,64]{2,1,0:T(1,128)S(1)} all-to-all(f32[8,1,64]{2,1,0:T(1,128)} %bitcast.41), channel_id=1, replica_groups=mesh['row'=8,'col'=32] {'row'}, dimensions={0} | all-to-all | bytes 4096 | tf_op jit(solution)/shard_map/all_to_all | solution.py:279
  214.8 0.5 add.435
  (52 shorter events, 0.4 us)
Async XLA Ops:
  7.2 87.2 %all-gather.3.cloned.1.call-start = ((), (), s32[]{:S(2)}) async-start(), calls=%async_computation.3 | async-start | bytes 10813440 | tf_op jit(solution)/shard_map/all_gather | solution.py:243
  9.2 43.5 %copy-start = (f32[64,2048]{1,0:T(8,128)}, f32[64,2048]{1,0:T(8,128)S(1)}, u32[]{:S(2)}) copy-start(f32[64,2048]{1,0:T(8,128)S(1)} %broadcast_multiply_fusion.masked_ref) | copy-start | bytes 1572868
  10.0 134.4 %reduce-scatter.2.cloned.1.call-start = ((), (), s32[]{:S(2)}) async-start(), calls=%async_computation.2 | async-start | bytes 3276800 | tf_op jit(solution)/shard_map/reduce_scatter | solution.py:264
  10.2 13.7 %collective-permute-start.3 = (f32[24,512]{1,0:T(8,128)S(1)}, f32[24,512]{1,0:T(8,128)S(1)}, u32[]{:S(2)}, u32[]{:S(2)}) collective-permute-start(f32[24,512]{1,0:T(8,128)S(1)} %get-tuple-element.65), channel_id=1, source_target_pairs={{0,3},{1,0},{2,1},{3,2},{4,35},{5,32},{6,33},{7,34},{8,67},{9,64},... | collective-permute-start | bytes 147464 | tf_op jit(solution)/shard_map/ppermute | solution.py:48
  12.2 11.6 %collective-permute-start.2 = (f32[24,512]{1,0:T(8,128)S(1)}, f32[24,512]{1,0:T(8,128)S(1)}, u32[]{:S(2)}, u32[]{:S(2)}) collective-permute-start(f32[24,512]{1,0:T(8,128)S(1)} %get-tuple-element.66), channel_id=1, source_target_pairs={{0,2},{1,3},{2,0},{3,1},{4,34},{5,35},{6,32},{7,33},{8,66},{9,67},... | collective-permute-start | bytes 147464 | tf_op jit(solution)/shard_map/ppermute | solution.py:48
  14.7 9.1 %collective-permute-start.1 = (f32[24,512]{1,0:T(8,128)S(1)}, f32[24,512]{1,0:T(8,128)S(1)}, u32[]{:S(2)}, u32[]{:S(2)}) collective-permute-start(f32[24,512]{1,0:T(8,128)S(1)} %get-tuple-element.67), channel_id=1, source_target_pairs={{0,1},{1,2},{2,3},{3,0},{4,33},{5,34},{6,35},{7,32},{8,65},{9,66},... | collective-permute-start | bytes 147464 | tf_op jit(solution)/shard_map/ppermute | solution.py:48
  19.4 11.4 %collective-permute-start = (f32[24,512]{1,0:T(8,128)S(1)}, f32[24,512]{1,0:T(8,128)S(1)}, u32[]{:S(2)}, u32[]{:S(2)}) collective-permute-start(f32[24,512]{1,0:T(8,128)S(1)} %get-tuple-element.68), channel_id=1, source_target_pairs={{0,0},{1,1},{2,2},{3,3},{4,32},{5,33},{6,34},{7,35},{8,64},{9,65},... | collective-permute-start | bytes 147464 | tf_op jit(solution)/shard_map/ppermute | solution.py:48
  30.8 18.7 %collective-permute-start.4 = (f32[4,24,512]{2,1,0:T(8,128)S(1)}, f32[4,24,512]{2,1,0:T(8,128)S(1)}, u32[]{:S(2)}, u32[]{:S(2)}) collective-permute-start(f32[4,24,512]{2,1,0:T(8,128)S(1)} %pad_maximum_fusion.3), channel_id=1, source_target_pairs={{0,128},{1,129},{2,130},{3,131},{4,132},{5,133},{6,134},{7,135},{8... | collective-permute-start | bytes 589832 | tf_op jit(solution)/shard_map/ppermute | solution.py:48
  52.6 23.9 %collective-permute-start.8 = (f32[1024,512]{1,0:T(8,128)}, f32[1024,512]{1,0:T(8,128)S(1)}, u32[]{:S(2)}, u32[]{:S(2)}) collective-permute-start(f32[1024,512]{1,0:T(8,128)} %constant_dynamic-slice_fusion), channel_id=1, source_target_pairs={{0,1},{1,0},{2,3},{3,2},{4,5},{5,4},{6,7},{7,6},{8,9},{9,8},{10,11... | collective-permute-start | bytes 6291464 | tf_op jit(solution)/shard_map/ppermute | solution.py:48
  52.6 11.9 %collective-permute-start.7 = (f32[8,24,512]{2,1,0:T(8,128)S(1)}, f32[8,24,512]{2,1,0:T(8,128)S(1)}, u32[]{:S(2)}, u32[]{:S(2)}) collective-permute-start(f32[8,24,512]{2,1,0:T(8,128)S(1)} %constant_dynamic-update-slice_fusion), channel_id=1, source_target_pairs={{0,96},{1,97},{2,98},{3,99},{4,100},{5,101},{6,102},{7,103},{8,104... | collective-permute-start | bytes 1179656 | tf_op jit(solution)/shard_map/ppermute | solution.py:48
  52.6 13.6 %collective-permute-start.6 = (f32[8,24,512]{2,1,0:T(8,128)S(1)}, f32[8,24,512]{2,1,0:T(8,128)S(1)}, u32[]{:S(2)}, u32[]{:S(2)}) collective-permute-start(f32[8,24,512]{2,1,0:T(8,128)S(1)} %constant_dynamic-update-slice_fusion), channel_id=1, source_target_pairs={{0,64},{1,65},{2,66},{3,67},{4,68},{5,69},{6,70},{7,71},{8,72},{9,... | collective-permute-start | bytes 1179656 | tf_op jit(solution)/shard_map/ppermute | solution.py:48
  52.7 21.5 %collective-permute-start.5 = (f32[8,24,512]{2,1,0:T(8,128)S(1)}, f32[8,24,512]{2,1,0:T(8,128)}, u32[]{:S(2)}, u32[]{:S(2)}) collective-permute-start(f32[8,24,512]{2,1,0:T(8,128)S(1)} %constant_dynamic-update-slice_fusion), channel_id=1, source_target_pairs={{0,32},{1,33},{2,34},{3,35},{4,36},{5,37},{6,38},{7,39},{8,40},{9,... | collective-permute-start | bytes 1179656 | tf_op jit(solution)/shard_map/ppermute | solution.py:48
  76.5 1.4 copy-start.1
  83.2 24.7 %collective-permute-start.9 = (f32[32,24,512]{2,1,0:T(8,128)}, f32[32,24,512]{2,1,0:T(8,128)S(1)}, u32[]{:S(2)}, u32[]{:S(2)}) collective-permute-start(f32[32,24,512]{2,1,0:T(8,128)} %pad_maximum_fusion.own_ref), channel_id=1, source_target_pairs={{0,1},{1,0},{2,3},{3,2},{4,5},{5,4},{6,7},{7,6},{8,9},{9,8},{10,11... | collective-permute-start | bytes 4718600 | tf_op jit(solution)/shard_map/ppermute | solution.py:48
  107.9 1.2 copy-start.10
  119.0 13.6 %copy-start.3 = (f32[8,24,1024]{2,1,0:T(8,128)S(1)}, f32[8,24,1024]{2,1,0:T(8,128)}, u32[]{:S(2)}) copy-start(f32[8,24,1024]{2,1,0:T(8,128)} %get-tuple-element.41) | copy-start | bytes 2359300
  119.0 11.5 %collective-permute-start.17 = (f32[4,24,1024]{2,1,0:T(8,128)}, f32[4,24,1024]{2,1,0:T(8,128)S(1)}, u32[]{:S(2)}, u32[]{:S(2)}) collective-permute-start(f32[4,24,1024]{2,1,0:T(8,128)} %get-tuple-element.44), channel_id=1, source_target_pairs={{0,6},{1,7},{2,0},{3,1},{4,2},{5,3},{6,4},{7,5},{8,14},{9,15},{10,... | collective-permute-start | bytes 1179656 | tf_op jit(solution)/shard_map/ppermute | solution.py:48
  119.8 12.8 %collective-permute-start.15 = (f32[4,24,1024]{2,1,0:T(8,128)}, f32[4,24,1024]{2,1,0:T(8,128)S(1)}, u32[]{:S(2)}, u32[]{:S(2)}) collective-permute-start(f32[4,24,1024]{2,1,0:T(8,128)} %get-tuple-element.42), channel_id=1, source_target_pairs={{0,2},{1,3},{2,4},{3,5},{4,6},{5,7},{6,0},{7,1},{8,10},{9,11},{10,... | collective-permute-start | bytes 1179656 | tf_op jit(solution)/shard_map/ppermute | solution.py:48
  131.8 19.4 %collective-permute-start.18 = (f32[8,24,1024]{2,1,0:T(8,128)S(1)}, f32[8,24,1024]{2,1,0:T(8,128)S(1)}, u32[]{:S(2)}, u32[]{:S(2)}) collective-permute-start(f32[8,24,1024]{2,1,0:T(8,128)S(1)} %pad_maximum_fusion.2), channel_id=1, source_target_pairs={{0,6},{1,7},{2,0},{3,1},{4,2},{5,3},{6,4},{7,5},{8,14},{9,15},{10,... | collective-permute-start | bytes 2359304 | tf_op jit(solution)/shard_map/ppermute | solution.py:48
  132.6 19.0 %copy-start.2 = (f32[8,24,1024]{2,1,0:T(8,128)S(1)}, f32[8,24,1024]{2,1,0:T(8,128)}, u32[]{:S(2)}) copy-start(f32[8,24,1024]{2,1,0:T(8,128)} %get-tuple-element.40) | copy-start | bytes 2359300
  132.8 18.9 %collective-permute-start.16 = (f32[8,24,1024]{2,1,0:T(8,128)S(1)}, f32[8,24,1024]{2,1,0:T(8,128)}, u32[]{:S(2)}, u32[]{:S(2)}) collective-permute-start(f32[8,24,1024]{2,1,0:T(8,128)S(1)} %pad_maximum_fusion.1), channel_id=1, source_target_pairs={{0,2},{1,3},{2,4},{3,5},{4,6},{5,7},{6,0},{7,1},{8,10},{9,11},{10,... | collective-permute-start | bytes 2359304 | tf_op jit(solution)/shard_map/ppermute | solution.py:48
  145.4 22.4 %collective-permute-start.10 = (f32[4,40,512]{2,1,0:T(8,128)S(1)}, f32[4,40,512]{2,1,0:T(8,128)S(1)}, u32[]{:S(2)}, u32[]{:S(2)}) collective-permute-start(f32[4,40,512]{2,1,0:T(8,128)S(1)} %slice.75), channel_id=1, source_target_pairs={{0,128},{1,129},{2,130},{3,131},{4,132},{5,133},{6,134},{7,135},{8... | collective-permute-start | bytes 983048 | tf_op jit(solution)/shard_map/ppermute | solution.py:48
  151.7 16.1 %copy-start.4 = (f32[8,40,512]{2,1,0:T(8,128)S(1)}, f32[8,40,512]{2,1,0:T(8,128)}, u32[]{:S(2)}) copy-start(f32[8,40,512]{2,1,0:T(8,128)} %reduce-scatter.2.cloned.1.call-done) | copy-start | bytes 1966084
  153.1 61.7 %copy-start.11 = (f32[64]{0:T(128)S(1)}, f32[64]{0:T(128)}, u32[]{:S(2)}) copy-start(f32[64]{0:T(128)} %param.7) | copy-start | bytes 772
  153.1 18.4 %collective-permute-start.19 = (f32[2,24,1024]{2,1,0:T(8,128)S(1)}, f32[2,24,1024]{2,1,0:T(8,128)S(1)}, u32[]{:S(2)}, u32[]{:S(2)}) collective-permute-start(f32[2,24,1024]{2,1,0:T(8,128)S(1)} %get-tuple-element.52), channel_id=1, source_target_pairs={{0,8},{1,9},{2,10},{3,11},{4,12},{5,13},{6,14},{7,15},{8,16},{9,17... | collective-permute-start | bytes 589832 | tf_op jit(solution)/shard_map/ppermute | solution.py:48
  154.3 19.8 %collective-permute-start.21 = (f32[2,24,1024]{2,1,0:T(8,128)S(1)}, f32[2,24,1024]{2,1,0:T(8,128)S(1)}, u32[]{:S(2)}, u32[]{:S(2)}) collective-permute-start(f32[2,24,1024]{2,1,0:T(8,128)S(1)} %get-tuple-element.53), channel_id=1, source_target_pairs={{0,24},{1,25},{2,26},{3,27},{4,28},{5,29},{6,30},{7,31},{8,0},{9,1... | collective-permute-start | bytes 589832 | tf_op jit(solution)/shard_map/ppermute | solution.py:48
  155.2 36.2 %collective-permute-start.20 = (f32[2,24,1024]{2,1,0:T(8,128)S(1)}, f32[2,24,1024]{2,1,0:T(8,128)S(1)}, u32[]{:S(2)}, u32[]{:S(2)}) collective-permute-start(f32[2,24,1024]{2,1,0:T(8,128)S(1)} %get-tuple-element.54), channel_id=1, source_target_pairs={{0,16},{1,17},{2,18},{3,19},{4,20},{5,21},{6,22},{7,23},{8,24},{9,... | collective-permute-start | bytes 589832 | tf_op jit(solution)/shard_map/ppermute | solution.py:48
  167.8 23.7 %collective-permute-start.14 = (f32[40,512]{1,0:T(8,128)S(1)}, f32[40,512]{1,0:T(8,128)S(1)}, u32[]{:S(2)}, u32[]{:S(2)}) collective-permute-start(f32[40,512]{1,0:T(8,128)S(1)} %get-tuple-element.59), channel_id=1, source_target_pairs={{0,3},{1,0},{2,1},{3,2},{4,35},{5,32},{6,33},{7,34},{8,67},{9,64},... | collective-permute-start | bytes 245768 | tf_op jit(solution)/shard_map/ppermute | solution.py:48
  167.9 23.6 %collective-permute-start.13 = (f32[40,512]{1,0:T(8,128)S(1)}, f32[40,512]{1,0:T(8,128)S(1)}, u32[]{:S(2)}, u32[]{:S(2)}) collective-permute-start(f32[40,512]{1,0:T(8,128)S(1)} %get-tuple-element.60), channel_id=1, source_target_pairs={{0,2},{1,3},{2,0},{3,1},{4,34},{5,35},{6,32},{7,33},{8,66},{9,67},... | collective-permute-start | bytes 245768 | tf_op jit(solution)/shard_map/ppermute | solution.py:48
  171.5 20.1 %collective-permute-start.12 = (f32[40,512]{1,0:T(8,128)S(1)}, f32[40,512]{1,0:T(8,128)S(1)}, u32[]{:S(2)}, u32[]{:S(2)}) collective-permute-start(f32[40,512]{1,0:T(8,128)S(1)} %get-tuple-element.61), channel_id=1, source_target_pairs={{0,1},{1,2},{2,3},{3,0},{4,33},{5,34},{6,35},{7,32},{8,65},{9,66},... | collective-permute-start | bytes 245768 | tf_op jit(solution)/shard_map/ppermute | solution.py:48
  174.2 17.4 %collective-permute-start.11 = (f32[40,512]{1,0:T(8,128)S(1)}, f32[40,512]{1,0:T(8,128)S(1)}, u32[]{:S(2)}, u32[]{:S(2)}) collective-permute-start(f32[40,512]{1,0:T(8,128)S(1)} %get-tuple-element.62), channel_id=1, source_target_pairs={{0,0},{1,1},{2,2},{3,3},{4,32},{5,33},{6,34},{7,35},{8,64},{9,65},... | collective-permute-start | bytes 245768 | tf_op jit(solution)/shard_map/ppermute | solution.py:48
  191.5 2.1 copy-start.6
  191.6 2.0 copy-start.7
  191.6 2.0 copy-start.8
  191.6 2.0 copy-start.9
  192.3 1.3 collective-permute-start.22
  193.6 0.6 copy-start.5
Sparse Core Ops, SparseCore 0:
  10.4 83.8 all-gather.2
  108.1 36.2 reduce-scatter.1

commit v3 on v2

--- a/solution.py
+++ b/solution.py
@@ -240,7 +240,7 @@
     mask = jnp.repeat(blocks, B, axis=1)
     masked = factor * mask
 
-    gathered = lax.all_gather(masked[:FIRST], "col")
+    gathered = lax.all_gather(factor[:FIRST] * mask, "col")
 
     rest = masked[FIRST:]
     rows = rest.shape[0]
@@ -266,15 +266,16 @@
     right = jnp.concatenate([right[:4] + send(far_right, along_x(1)), right[4:]])
     left = jnp.concatenate([left[:4], left[4:] + send(far_left, along_x(-1))])
     here = here + send(right, along_x(1)) + send(left, along_x(-1))
+    shift = jnp.concatenate([(col - jnp.arange(4, dtype=jnp.int32)) % 4, jnp.stack([core, 1 - core])])
+    first, shift = tie(first, shift)
     first = sum_zh(first)
     groups = [send(first[n], regroup(n)) for n in range(4)]
     total = here[:2]
     for n in (1, 2, 3):
         total = total + send(here[2 * n : 2 * n + 2], along_zl(n))
-    *groups, total = tie(*groups, total)
+    groups[3], total = tie(groups[3], total)
     groups += [total[0], send(total[1], OTHER_CORE)]
 
-    shift = jnp.concatenate([(col - jnp.arange(4, dtype=jnp.int32)) % 4, jnp.stack([core, 1 - core])])
     sigma_off, shares = finish(shift, mask, masked, groups)
     shares = lax.all_to_all(shares, "row", 0, 0, tiled=True)
     return sigma_off, base_var + jnp.sum(shares, axis=0)

time: 225 us -> 237 us (1.053)
  blocking collectives: 18.5 us -> 25.6 us
  waiting for transfers between devices: 81.7 us -> 87.4 us
    all_to_all x1, blocking collectives: 18.5 us -> 25.6 us  [body(): shares = lax.all_to_all(shares, 'row', 0, 0, tiled=True)]
    ppermute x23, waiting for transfers between devices: 61.6 us -> 67.8 us  [send(): return lax.ppermute(value, AXES, perm)]
  transfers between devices with their start and end apart: 25 -> 25, of which waited for: 14 -> 15; matrix products, arithmetic and copies ran while one was open for 5% -> 6% of each run, Pallas kernels for 16% -> 15%
where the time goes in v3:
time: 237 us; the launch traced here: 236 us
  waiting for transfers between devices  87.4 us (37%)
  starting transfers between devices  51.3 us (22%)
  Pallas kernels  37.7 us (16%)
  blocking collectives  25.6 us (11%)
  between operations  14.5 us (6%)
  other arithmetic  11.4 us (5%)
  local copies, waits for them, and re-layouts  8.02 us (3%)
    ppermute x23, waiting for transfers between devices, send(): return lax.ppermute(value, AXES, perm)  67.8 us
    ppermute x23, starting transfers between devices, send(): return lax.ppermute(value, AXES, perm)  51.3 us
    all_to_all x1, blocking collectives, body(): shares = lax.all_to_all(shares, 'row', 0, 0, tiled=True)  25.6 us
    pallas_call x1, Pallas kernels, whole_products(): pl.pallas_call(whole_kernel, grid=(blocks // group,), in_specs=[pl.BlockS...  13.6 us
    pallas_call x1, Pallas kernels, turned_products(): pl.pallas_call(turned_kernel, in_specs=[pl.BlockSpec(memory_space=pltpu.S...  9.91 us
    all_gather x1, waiting for transfers between devices, body(): gathered = lax.all_gather(factor[:FIRST] * mask, 'col')  9.86 us
    reduce_scatter x1, waiting for transfers between devices, body(): lax.psum_scatter(first, 'row', scatter_dimension=0, axis_index_groups=pai...  9.7 us
    pallas_call x1, Pallas kernels, split_all(): pl.pallas_call(split_kernel, grid=(value.shape[0] // 256,), in_specs=[spe...  6.83 us
  transfers between devices with their start and end apart: 25, of which 15 were waited for; matrix products, arithmetic and copies ran while one was open for 6% of the time, Pallas kernels for 15%

profile of v3, /device:TPU:36, one launch (start us, length us, event | category | flops | bytes accessed | tf_op | source)
XLA Modules:
  0.0 236.0 jit_solution(15889561984098640006)
XLA Ops:
  7.2 0.8 convert_bitcast_fusion
  8.0 0.1 broadcast_bitcast_fusion
  8.1 1.7 slice_multiply_fusion
  9.8 0.0 reduce-scatter.2.cloned.1.call-start
  9.9 1.1 broadcast_multiply_fusion.masked_ref
  11.1 2.0 collective-permute-start.3
  13.2 2.5 %collective-permute-start.2 = (f32[24,512]{1,0:T(8,128)S(1)}, f32[24,512]{1,0:T(8,128)S(1)}, u32[]{:S(2)}, u32[]{:S(2)}) collective-permute-start(f32[24,512]{1,0:T(8,128)S(1)} %get-tuple-element.64), channel_id=1, source_target_pairs={{0,2},{1,3},{2,0},{3,1},{4,34},{5,35},{6,32},{7,33},{8,66},{9,67},... | collective-permute-start | bytes 147464 | tf_op jit(solution)/shard_map/ppermute | solution.py:48
  15.7 4.6 %collective-permute-start.1 = (f32[24,512]{1,0:T(8,128)S(1)}, f32[24,512]{1,0:T(8,128)S(1)}, u32[]{:S(2)}, u32[]{:S(2)}) collective-permute-start(f32[24,512]{1,0:T(8,128)S(1)} %get-tuple-element.65), channel_id=1, source_target_pairs={{0,1},{1,2},{2,3},{3,0},{4,33},{5,34},{6,35},{7,32},{8,65},{9,66},... | collective-permute-start | bytes 147464 | tf_op jit(solution)/shard_map/ppermute | solution.py:48
  20.3 4.4 %collective-permute-start = (f32[24,512]{1,0:T(8,128)S(1)}, f32[24,512]{1,0:T(8,128)S(1)}, u32[]{:S(2)}, u32[]{:S(2)}) collective-permute-start(f32[24,512]{1,0:T(8,128)S(1)} %get-tuple-element.66), channel_id=1, source_target_pairs={{0,0},{1,1},{2,2},{3,3},{4,32},{5,33},{6,34},{7,35},{8,64},{9,65},... | collective-permute-start | bytes 147464 | tf_op jit(solution)/shard_map/ppermute | solution.py:48
  24.8 7.0 %collective-permute-done = f32[24,512]{1,0:T(8,128)S(1)} collective-permute-done((f32[24,512]{1,0:T(8,128)S(1)}, f32[24,512]{1,0:T(8,128)S(1)}, u32[]{:S(2)}, u32[]{:S(2)}) %collective-permute-start) | collective-permute-done | bytes 49184 | tf_op jit(solution)/shard_map/ppermute | solution.py:48
  31.8 12.4 %collective-permute-start.4 = (f32[4,24,512]{2,1,0:T(8,128)S(1)}, f32[4,24,512]{2,1,0:T(8,128)S(1)}, u32[]{:S(2)}, u32[]{:S(2)}) collective-permute-start(f32[4,24,512]{2,1,0:T(8,128)S(1)} %pad_maximum_fusion.3), channel_id=1, source_target_pairs={{0,128},{1,129},{2,130},{3,131},{4,132},{5,133},{6,134},{7,135},{8... | collective-permute-start | bytes 589832 | tf_op jit(solution)/shard_map/ppermute | solution.py:48
  44.3 6.0 %collective-permute-done.4 = f32[4,24,512]{2,1,0:T(8,128)S(1)} collective-permute-done((f32[4,24,512]{2,1,0:T(8,128)S(1)}, f32[4,24,512]{2,1,0:T(8,128)S(1)}, u32[]{:S(2)}, u32[]{:S(2)}) %collective-permute-start.4) | collective-permute-done | bytes 196640 | tf_op jit(solution)/shard_map/ppermute | solution.py:48
  50.3 3.2 %constant_dynamic-slice_fusion = f32[1024,512]{1,0:T(8,128)} fusion(f32[2048,512]{1,0:T(8,128)} %own_ref, s32[]{:T(128)S(6)} %select_n.325), kind=kLoop, calls=%fused_computation.66 | loop fusion | bytes 4194308 | tf_op jit(solution)/shard_map/dynamic_slice | solution.py:254
  53.5 0.1 collective-permute-start.6
  53.6 1.9 collective-permute-start.5
  55.5 6.8 %split_sigma.1 = (bf16[2048,512]{1,0:T(8,128)(2,1)}, bf16[2048,512]{1,0:T(8,128)(2,1)}) custom-call(f32[2048,512]{1,0:T(8,128)} %own_ref), custom_call_target="tpu_custom_call" | custom-call | tf_op jit(solution)/shard_map/split_sigma/pallas_call | solution.py:66
  62.3 3.1 %collective-permute-done.7 = f32[8,24,512]{2,1,0:T(8,128)S(1)} collective-permute-done((f32[8,24,512]{2,1,0:T(8,128)S(1)}, f32[8,24,512]{2,1,0:T(8,128)S(1)}, u32[]{:S(2)}, u32[]{:S(2)}) %collective-permute-start.7) | collective-permute-done | bytes 393248 | tf_op jit(solution)/shard_map/ppermute | solution.py:48
  65.4 1.7 collective-permute-done.6
  67.0 8.0 %collective-permute-done.5 = f32[8,24,512]{2,1,0:T(8,128)} collective-permute-done((f32[8,24,512]{2,1,0:T(8,128)S(1)}, f32[8,24,512]{2,1,0:T(8,128)}, u32[]{:S(2)}, u32[]{:S(2)}) %collective-permute-start.5) | collective-permute-done | bytes 393248 | tf_op jit(solution)/shard_map/ppermute | solution.py:48
  75.1 2.3 pad_maximum_fusion.own_ref
  77.4 1.4 copy-done.1
  78.8 5.3 %turn_sigma.1 = (bf16[1024,1024]{1,0:T(8,128)(2,1)}, bf16[1024,1024]{1,0:T(8,128)(2,1)}) custom-call(s32[1]{0:T(128)} %bitcast.6.core_ref, f32[2048,512]{1,0:T(8,128)} %own_ref, f32[1024,512]{1,0:T(8,128)} %copy-done.1), custom_call_target="tpu_custom_call" | custom-call | tf_op jit(solution)/shard_map/turn_sigma/pallas_call | solution.py:124
  84.1 0.0 collective-permute-start.9
  84.2 0.6 fusion.3.tab_ref
  84.8 9.9 %all-gather.3.cloned.1.call-done = f32[1280,2048]{1,0:T(8,128)} async-done(((f32[40,2048]{1,0:T(8,128)}), f32[1280,2048]{1,0:T(8,128)}) %all-gather.3.cloned.1.call-update) | async-done | bytes 10485776 | tf_op jit(solution)/shard_map/all_gather | solution.py:243
  94.6 13.6 %whole_products.1 = f32[32,40,512]{2,1,0:T(8,128)} custom-call(s32[32]{0:T(128)} %fusion.3.tab_ref, f32[32,40,2048]{2,1,0:T(8,128)} %bitcast.43, bf16[2048,512]{1,0:T(8,128)(2,1)} %get-tuple-element.32.sh_ref, bf16[2048,512]{1,0:T(8,128)(2,1)} %get-tuple-element.33.sl_ref), custom_call_target="tpu_custom_call" | custom-call | flops 8053063680 | bytes 18874368 | tf_op jit(solution)/shard_map/whole_products/pallas_call | solution.py:94
  108.3 0.8 pad_add_fusion.tab_ref
  109.1 0.3 copy-done.10
  109.4 9.9 %turned_products.1 = (f32[8,24,1024]{2,1,0:T(8,128)}, f32[8,24,1024]{2,1,0:T(8,128)}, f32[4,24,1024]{2,1,0:T(8,128)}, f32[4,24,1024]{2,1,0:T(8,128)}, f32[8,24,1024]{2,1,0:T(8,128)}) custom-call(s32[2,32]{1,0:T(2,128)} %pad_add_fusion.tab_ref, f32[32,24,512]{2,1,0:T(8,128)} %pad_maximum_fusion.own_ref, f32[32,24,512]{2,1,0:T(8,128)} %copy-done.10, ...), custom_call_target="tpu_custom_call" | custom-call | flops 4831838208 | bytes 10485760 | tf_op jit(solution)/shard_map/turned_products/pallas_call | solution.py:166
  119.3 1.3 collective-permute-start.17
  120.6 0.7 collective-permute-start.15
  121.3 9.4 %collective-permute-done.17 = f32[4,24,1024]{2,1,0:T(8,128)S(1)} collective-permute-done((f32[4,24,1024]{2,1,0:T(8,128)}, f32[4,24,1024]{2,1,0:T(8,128)S(1)}, u32[]{:S(2)}, u32[]{:S(2)}) %collective-permute-start.17) | collective-permute-done | bytes 393248 | tf_op jit(solution)/shard_map/ppermute | solution.py:48
  130.8 1.2 fusion.30
  132.0 0.1 pad_maximum_fusion.2
  132.0 1.4 collective-permute-start.18
  133.4 0.1 slice_add_fusion.1
  133.5 0.1 pad_maximum_fusion.1
  133.6 1.0 collective-permute-start.16
  134.6 0.7 pad_add_fusion.1.shift_ref
  135.3 9.7 %reduce-scatter.2.cloned.1.call-done = f32[8,40,512]{2,1,0:T(8,128)} async-done(((f32[32,40,512]{2,1,0:T(8,128)}), f32[8,40,512]{2,1,0:T(8,128)}) %reduce-scatter.2.cloned.1.call-update) | async-done | bytes 655376 | tf_op jit(solution)/shard_map/reduce_scatter | solution.py:264
  145.0 1.0 slice.57
  146.0 4.9 %collective-permute-start.10 = (f32[4,40,512]{2,1,0:T(8,128)S(1)}, f32[4,40,512]{2,1,0:T(8,128)S(1)}, u32[]{:S(2)}, u32[]{:S(2)}) collective-permute-start(f32[4,40,512]{2,1,0:T(8,128)S(1)} %slice.57), channel_id=1, source_target_pairs={{0,128},{1,129},{2,130},{3,131},{4,132},{5,133},{6,134},{7,135},{8... | collective-permute-start | bytes 983048 | tf_op jit(solution)/shard_map/ppermute | solution.py:48
  150.9 0.6 collective-permute-done.18
  151.5 0.9 collective-permute-done.16
  152.5 1.4 add_add_fusion
  153.9 1.3 collective-permute-start.19
  155.3 0.8 collective-permute-start.21
  156.0 1.2 collective-permute-start.20
  157.2 11.2 %collective-permute-done.10 = f32[4,40,512]{2,1,0:T(8,128)S(1)} collective-permute-done((f32[4,40,512]{2,1,0:T(8,128)S(1)}, f32[4,40,512]{2,1,0:T(8,128)S(1)}, u32[]{:S(2)}, u32[]{:S(2)}) %collective-permute-start.10) | collective-permute-done | bytes 327712 | tf_op jit(solution)/shard_map/ppermute | solution.py:48
  168.6 0.1 collective-permute-start.14
  168.6 3.4 %collective-permute-done.19 = f32[2,24,1024]{2,1,0:T(8,128)S(1)} collective-permute-done((f32[2,24,1024]{2,1,0:T(8,128)S(1)}, f32[2,24,1024]{2,1,0:T(8,128)S(1)}, u32[]{:S(2)}, u32[]{:S(2)}) %collective-permute-start.19) | collective-permute-done | bytes 196640 | tf_op jit(solution)/shard_map/ppermute | solution.py:48
  172.1 2.6 %collective-permute-done.21 = f32[2,24,1024]{2,1,0:T(8,128)S(1)} collective-permute-done((f32[2,24,1024]{2,1,0:T(8,128)S(1)}, f32[2,24,1024]{2,1,0:T(8,128)S(1)}, u32[]{:S(2)}, u32[]{:S(2)}) %collective-permute-start.21) | collective-permute-done | bytes 196640 | tf_op jit(solution)/shard_map/ppermute | solution.py:48
  174.7 7.9 %collective-permute-done.20 = f32[2,24,1024]{2,1,0:T(8,128)S(1)} collective-permute-done((f32[2,24,1024]{2,1,0:T(8,128)S(1)}, f32[2,24,1024]{2,1,0:T(8,128)S(1)}, u32[]{:S(2)}, u32[]{:S(2)}) %collective-permute-start.20) | collective-permute-done | bytes 196640 | tf_op jit(solution)/shard_map/ppermute | solution.py:48
  182.6 0.1 fusion.1
  182.7 0.7 slice_bitcast_fusion
  183.4 2.2 collective-permute-start.13
  185.5 3.9 %collective-permute-start.12 = (f32[40,512]{1,0:T(8,128)S(1)}, f32[40,512]{1,0:T(8,128)S(1)}, u32[]{:S(2)}, u32[]{:S(2)}) collective-permute-start(f32[40,512]{1,0:T(8,128)S(1)} %get-tuple-element.59), channel_id=1, source_target_pairs={{0,1},{1,2},{2,3},{3,0},{4,33},{5,34},{6,35},{7,32},{8,65},{9,66},... | collective-permute-start | bytes 245768 | tf_op jit(solution)/shard_map/ppermute | solution.py:48
  189.4 4.4 %collective-permute-start.11 = (f32[40,512]{1,0:T(8,128)S(1)}, f32[40,512]{1,0:T(8,128)S(1)}, u32[]{:S(2)}, u32[]{:S(2)}) collective-permute-start(f32[40,512]{1,0:T(8,128)S(1)} %get-tuple-element.60), channel_id=1, source_target_pairs={{0,0},{1,1},{2,2},{3,3},{4,32},{5,33},{6,34},{7,35},{8,64},{9,65},... | collective-permute-start | bytes 245768 | tf_op jit(solution)/shard_map/ppermute | solution.py:48
  193.8 0.6 copy.8
  194.4 5.8 %collective-permute-done.11.refs_0_ = f32[40,512]{1,0:T(8,128)S(1)} collective-permute-done((f32[40,512]{1,0:T(8,128)S(1)}, f32[40,512]{1,0:T(8,128)S(1)}, u32[]{:S(2)}, u32[]{:S(2)}) %collective-permute-start.11) | collective-permute-done | bytes 81952 | tf_op jit(solution)/shard_map/ppermute | solution.py:48
  200.3 0.6 copy-done.9
  200.9 2.1 finish.1
  203.0 25.6 %all_to_all.9 = f32[8,1,64]{2,1,0:T(1,128)S(1)} all-to-all(f32[8,1,64]{2,1,0:T(1,128)} %bitcast.42), channel_id=1, replica_groups=mesh['row'=8,'col'=32] {'row'}, dimensions={0} | all-to-all | bytes 4096 | tf_op jit(solution)/shard_map/all_to_all | solution.py:280
  228.6 0.5 add.435
  (52 shorter events, 0.5 us)
Async XLA Ops:
  7.2 87.5 %all-gather.3.cloned.1.call-start = ((), (), s32[]{:S(2)}) async-start(), calls=%async_computation.3 | async-start | bytes 10813440 | tf_op jit(solution)/shard_map/all_gather | solution.py:243
  9.8 135.1 %reduce-scatter.2.cloned.1.call-start = ((), (), s32[]{:S(2)}) async-start(), calls=%async_computation.2 | async-start | bytes 3276800 | tf_op jit(solution)/shard_map/reduce_scatter | solution.py:264
  11.0 42.4 %copy-start = (f32[64,2048]{1,0:T(8,128)}, f32[64,2048]{1,0:T(8,128)S(1)}, u32[]{:S(2)}) copy-start(f32[64,2048]{1,0:T(8,128)S(1)} %broadcast_multiply_fusion.masked_ref) | copy-start | bytes 1572868
  11.1 13.7 %collective-permute-start.3 = (f32[24,512]{1,0:T(8,128)S(1)}, f32[24,512]{1,0:T(8,128)S(1)}, u32[]{:S(2)}, u32[]{:S(2)}) collective-permute-start(f32[24,512]{1,0:T(8,128)S(1)} %get-tuple-element.63), channel_id=1, source_target_pairs={{0,3},{1,0},{2,1},{3,2},{4,35},{5,32},{6,33},{7,34},{8,67},{9,64},... | collective-permute-start | bytes 147464 | tf_op jit(solution)/shard_map/ppermute | solution.py:48
  13.2 11.6 %collective-permute-start.2 = (f32[24,512]{1,0:T(8,128)S(1)}, f32[24,512]{1,0:T(8,128)S(1)}, u32[]{:S(2)}, u32[]{:S(2)}) collective-permute-start(f32[24,512]{1,0:T(8,128)S(1)} %get-tuple-element.64), channel_id=1, source_target_pairs={{0,2},{1,3},{2,0},{3,1},{4,34},{5,35},{6,32},{7,33},{8,66},{9,67},... | collective-permute-start | bytes 147464 | tf_op jit(solution)/shard_map/ppermute | solution.py:48
  15.7 9.1 %collective-permute-start.1 = (f32[24,512]{1,0:T(8,128)S(1)}, f32[24,512]{1,0:T(8,128)S(1)}, u32[]{:S(2)}, u32[]{:S(2)}) collective-permute-start(f32[24,512]{1,0:T(8,128)S(1)} %get-tuple-element.65), channel_id=1, source_target_pairs={{0,1},{1,2},{2,3},{3,0},{4,33},{5,34},{6,35},{7,32},{8,65},{9,66},... | collective-permute-start | bytes 147464 | tf_op jit(solution)/shard_map/ppermute | solution.py:48
  20.3 11.5 %collective-permute-start = (f32[24,512]{1,0:T(8,128)S(1)}, f32[24,512]{1,0:T(8,128)S(1)}, u32[]{:S(2)}, u32[]{:S(2)}) collective-permute-start(f32[24,512]{1,0:T(8,128)S(1)} %get-tuple-element.66), channel_id=1, source_target_pairs={{0,0},{1,1},{2,2},{3,3},{4,32},{5,33},{6,34},{7,35},{8,64},{9,65},... | collective-permute-start | bytes 147464 | tf_op jit(solution)/shard_map/ppermute | solution.py:48
  31.8 18.5 %collective-permute-start.4 = (f32[4,24,512]{2,1,0:T(8,128)S(1)}, f32[4,24,512]{2,1,0:T(8,128)S(1)}, u32[]{:S(2)}, u32[]{:S(2)}) collective-permute-start(f32[4,24,512]{2,1,0:T(8,128)S(1)} %pad_maximum_fusion.3), channel_id=1, source_target_pairs={{0,128},{1,129},{2,130},{3,131},{4,132},{5,133},{6,134},{7,135},{8... | collective-permute-start | bytes 589832 | tf_op jit(solution)/shard_map/ppermute | solution.py:48
  53.5 23.9 %collective-permute-start.8 = (f32[1024,512]{1,0:T(8,128)}, f32[1024,512]{1,0:T(8,128)S(1)}, u32[]{:S(2)}, u32[]{:S(2)}) collective-permute-start(f32[1024,512]{1,0:T(8,128)} %constant_dynamic-slice_fusion), channel_id=1, source_target_pairs={{0,1},{1,0},{2,3},{3,2},{4,5},{5,4},{6,7},{7,6},{8,9},{9,8},{10,11... | collective-permute-start | bytes 6291464 | tf_op jit(solution)/shard_map/ppermute | solution.py:48
  53.5 11.9 %collective-permute-start.7 = (f32[8,24,512]{2,1,0:T(8,128)S(1)}, f32[8,24,512]{2,1,0:T(8,128)S(1)}, u32[]{:S(2)}, u32[]{:S(2)}) collective-permute-start(f32[8,24,512]{2,1,0:T(8,128)S(1)} %constant_dynamic-update-slice_fusion), channel_id=1, source_target_pairs={{0,96},{1,97},{2,98},{3,99},{4,100},{5,101},{6,102},{7,103},{8,104... | collective-permute-start | bytes 1179656 | tf_op jit(solution)/shard_map/ppermute | solution.py:48
  53.5 13.6 %collective-permute-start.6 = (f32[8,24,512]{2,1,0:T(8,128)S(1)}, f32[8,24,512]{2,1,0:T(8,128)S(1)}, u32[]{:S(2)}, u32[]{:S(2)}) collective-permute-start(f32[8,24,512]{2,1,0:T(8,128)S(1)} %constant_dynamic-update-slice_fusion), channel_id=1, source_target_pairs={{0,64},{1,65},{2,66},{3,67},{4,68},{5,69},{6,70},{7,71},{8,72},{9,... | collective-permute-start | bytes 1179656 | tf_op jit(solution)/shard_map/ppermute | solution.py:48
  53.6 21.5 %collective-permute-start.5 = (f32[8,24,512]{2,1,0:T(8,128)S(1)}, f32[8,24,512]{2,1,0:T(8,128)}, u32[]{:S(2)}, u32[]{:S(2)}) collective-permute-start(f32[8,24,512]{2,1,0:T(8,128)S(1)} %constant_dynamic-update-slice_fusion), channel_id=1, source_target_pairs={{0,32},{1,33},{2,34},{3,35},{4,36},{5,37},{6,38},{7,39},{8,40},{9,... | collective-permute-start | bytes 1179656 | tf_op jit(solution)/shard_map/ppermute | solution.py:48
  77.4 1.4 copy-start.1
  84.1 24.1 %collective-permute-start.9 = (f32[32,24,512]{2,1,0:T(8,128)}, f32[32,24,512]{2,1,0:T(8,128)S(1)}, u32[]{:S(2)}, u32[]{:S(2)}) collective-permute-start(f32[32,24,512]{2,1,0:T(8,128)} %pad_maximum_fusion.own_ref), channel_id=1, source_target_pairs={{0,1},{1,0},{2,3},{3,2},{4,5},{5,4},{6,7},{7,6},{8,9},{9,8},{10,11... | collective-permute-start | bytes 4718600 | tf_op jit(solution)/shard_map/ppermute | solution.py:48
  108.2 1.2 copy-start.10
  119.3 14.2 %copy-start.3 = (f32[8,24,1024]{2,1,0:T(8,128)S(1)}, f32[8,24,1024]{2,1,0:T(8,128)}, u32[]{:S(2)}) copy-start(f32[8,24,1024]{2,1,0:T(8,128)} %get-tuple-element.42) | copy-start | bytes 2359300
  119.3 11.5 %collective-permute-start.17 = (f32[4,24,1024]{2,1,0:T(8,128)}, f32[4,24,1024]{2,1,0:T(8,128)S(1)}, u32[]{:S(2)}, u32[]{:S(2)}) collective-permute-start(f32[4,24,1024]{2,1,0:T(8,128)} %get-tuple-element.45), channel_id=1, source_target_pairs={{0,6},{1,7},{2,0},{3,1},{4,2},{5,3},{6,4},{7,5},{8,14},{9,15},{10,... | collective-permute-start | bytes 1179656 | tf_op jit(solution)/shard_map/ppermute | solution.py:48
  120.6 12.8 %collective-permute-start.15 = (f32[4,24,1024]{2,1,0:T(8,128)}, f32[4,24,1024]{2,1,0:T(8,128)S(1)}, u32[]{:S(2)}, u32[]{:S(2)}) collective-permute-start(f32[4,24,1024]{2,1,0:T(8,128)} %get-tuple-element.43), channel_id=1, source_target_pairs={{0,2},{1,3},{2,4},{3,5},{4,6},{5,7},{6,0},{7,1},{8,10},{9,11},{10,... | collective-permute-start | bytes 1179656 | tf_op jit(solution)/shard_map/ppermute | solution.py:48
  132.0 19.5 %collective-permute-start.18 = (f32[8,24,1024]{2,1,0:T(8,128)S(1)}, f32[8,24,1024]{2,1,0:T(8,128)S(1)}, u32[]{:S(2)}, u32[]{:S(2)}) collective-permute-start(f32[8,24,1024]{2,1,0:T(8,128)S(1)} %pad_maximum_fusion.2), channel_id=1, source_target_pairs={{0,6},{1,7},{2,0},{3,1},{4,2},{5,3},{6,4},{7,5},{8,14},{9,15},{10,... | collective-permute-start | bytes 2359304 | tf_op jit(solution)/shard_map/ppermute | solution.py:48
  133.4 19.0 %copy-start.2 = (f32[8,24,1024]{2,1,0:T(8,128)S(1)}, f32[8,24,1024]{2,1,0:T(8,128)}, u32[]{:S(2)}) copy-start(f32[8,24,1024]{2,1,0:T(8,128)} %get-tuple-element.41) | copy-start | bytes 2359300
  133.6 18.9 %collective-permute-start.16 = (f32[8,24,1024]{2,1,0:T(8,128)S(1)}, f32[8,24,1024]{2,1,0:T(8,128)}, u32[]{:S(2)}, u32[]{:S(2)}) collective-permute-start(f32[8,24,1024]{2,1,0:T(8,128)S(1)} %pad_maximum_fusion.1), channel_id=1, source_target_pairs={{0,2},{1,3},{2,4},{3,5},{4,6},{5,7},{6,0},{7,1},{8,10},{9,11},{10,... | collective-permute-start | bytes 2359304 | tf_op jit(solution)/shard_map/ppermute | solution.py:48
  146.0 22.5 %collective-permute-start.10 = (f32[4,40,512]{2,1,0:T(8,128)S(1)}, f32[4,40,512]{2,1,0:T(8,128)S(1)}, u32[]{:S(2)}, u32[]{:S(2)}) collective-permute-start(f32[4,40,512]{2,1,0:T(8,128)S(1)} %slice.57), channel_id=1, source_target_pairs={{0,128},{1,129},{2,130},{3,131},{4,132},{5,133},{6,134},{7,135},{8... | collective-permute-start | bytes 983048 | tf_op jit(solution)/shard_map/ppermute | solution.py:48
  152.5 16.0 %copy-start.4 = (f32[8,40,512]{2,1,0:T(8,128)S(1)}, f32[8,40,512]{2,1,0:T(8,128)}, u32[]{:S(2)}) copy-start(f32[8,40,512]{2,1,0:T(8,128)} %reduce-scatter.2.cloned.1.call-done) | copy-start | bytes 1966084
  153.9 74.7 %copy-start.11 = (f32[64]{0:T(128)S(1)}, f32[64]{0:T(128)}, u32[]{:S(2)}) copy-start(f32[64]{0:T(128)} %param.7) | copy-start | bytes 772
  153.9 18.2 %collective-permute-start.19 = (f32[2,24,1024]{2,1,0:T(8,128)S(1)}, f32[2,24,1024]{2,1,0:T(8,128)S(1)}, u32[]{:S(2)}, u32[]{:S(2)}) collective-permute-start(f32[2,24,1024]{2,1,0:T(8,128)S(1)} %get-tuple-element.50), channel_id=1, source_target_pairs={{0,8},{1,9},{2,10},{3,11},{4,12},{5,13},{6,14},{7,15},{8,16},{9,17... | collective-permute-start | bytes 589832 | tf_op jit(solution)/shard_map/ppermute | solution.py:48
  155.3 19.4 %collective-permute-start.21 = (f32[2,24,1024]{2,1,0:T(8,128)S(1)}, f32[2,24,1024]{2,1,0:T(8,128)S(1)}, u32[]{:S(2)}, u32[]{:S(2)}) collective-permute-start(f32[2,24,1024]{2,1,0:T(8,128)S(1)} %get-tuple-element.51), channel_id=1, source_target_pairs={{0,24},{1,25},{2,26},{3,27},{4,28},{5,29},{6,30},{7,31},{8,0},{9,1... | collective-permute-start | bytes 589832 | tf_op jit(solution)/shard_map/ppermute | solution.py:48
  156.0 26.6 %collective-permute-start.20 = (f32[2,24,1024]{2,1,0:T(8,128)S(1)}, f32[2,24,1024]{2,1,0:T(8,128)S(1)}, u32[]{:S(2)}, u32[]{:S(2)}) collective-permute-start(f32[2,24,1024]{2,1,0:T(8,128)S(1)} %get-tuple-element.52), channel_id=1, source_target_pairs={{0,16},{1,17},{2,18},{3,19},{4,20},{5,21},{6,22},{7,23},{8,24},{9,... | collective-permute-start | bytes 589832 | tf_op jit(solution)/shard_map/ppermute | solution.py:48
  168.6 14.1 %collective-permute-start.14 = (f32[40,512]{1,0:T(8,128)S(1)}, f32[40,512]{1,0:T(8,128)S(1)}, u32[]{:S(2)}, u32[]{:S(2)}) collective-permute-start(f32[40,512]{1,0:T(8,128)S(1)} %get-tuple-element.57), channel_id=1, source_target_pairs={{0,3},{1,0},{2,1},{3,2},{4,35},{5,32},{6,33},{7,34},{8,67},{9,64},... | collective-permute-start | bytes 245768 | tf_op jit(solution)/shard_map/ppermute | solution.py:48
  182.7 17.6 %copy-start.6 = (f32[40,512]{1,0:T(8,128)}, f32[40,512]{1,0:T(8,128)S(1)}, u32[]{:S(2)}) copy-start(f32[40,512]{1,0:T(8,128)S(1)} %collective-permute-done.14.refs_3_) | copy-start | bytes 245764
  183.3 16.9 %collective-permute-start.22 = (f32[24,1024]{1,0:T(8,128)S(1)}, f32[24,1024]{1,0:T(8,128)S(1)}, u32[]{:S(2)}, u32[]{:S(2)}) collective-permute-start(f32[24,1024]{1,0:T(8,128)S(1)} %get-tuple-element.61), channel_id=1, source_target_pairs={{0,1},{1,0},{2,3},{3,2},{4,5},{5,4},{6,7},{7,6},{8,9},{9,8},{10,11... | collective-permute-start | bytes 294920 | tf_op jit(solution)/shard_map/ppermute | solution.py:48
  183.4 11.1 %collective-permute-start.13 = (f32[40,512]{1,0:T(8,128)S(1)}, f32[40,512]{1,0:T(8,128)S(1)}, u32[]{:S(2)}, u32[]{:S(2)}) collective-permute-start(f32[40,512]{1,0:T(8,128)S(1)} %get-tuple-element.58), channel_id=1, source_target_pairs={{0,2},{1,3},{2,0},{3,1},{4,34},{5,35},{6,32},{7,33},{8,66},{9,67},... | collective-permute-start | bytes 245768 | tf_op jit(solution)/shard_map/ppermute | solution.py:48
  185.5 8.9 %collective-permute-start.12 = (f32[40,512]{1,0:T(8,128)S(1)}, f32[40,512]{1,0:T(8,128)S(1)}, u32[]{:S(2)}, u32[]{:S(2)}) collective-permute-start(f32[40,512]{1,0:T(8,128)S(1)} %get-tuple-element.59), channel_id=1, source_target_pairs={{0,1},{1,2},{2,3},{3,0},{4,33},{5,34},{6,35},{7,32},{8,65},{9,66},... | collective-permute-start | bytes 245768 | tf_op jit(solution)/shard_map/ppermute | solution.py:48
  189.4 10.8 %collective-permute-start.11 = (f32[40,512]{1,0:T(8,128)S(1)}, f32[40,512]{1,0:T(8,128)S(1)}, u32[]{:S(2)}, u32[]{:S(2)}) collective-permute-start(f32[40,512]{1,0:T(8,128)S(1)} %get-tuple-element.60), channel_id=1, source_target_pairs={{0,0},{1,1},{2,2},{3,3},{4,32},{5,33},{6,34},{7,35},{8,64},{9,65},... | collective-permute-start | bytes 245768 | tf_op jit(solution)/shard_map/ppermute | solution.py:48
  194.4 5.9 %copy-start.7 = (f32[40,512]{1,0:T(8,128)}, f32[40,512]{1,0:T(8,128)S(1)}, u32[]{:S(2)}) copy-start(f32[40,512]{1,0:T(8,128)S(1)} %collective-permute-done.13.refs_2_) | copy-start | bytes 245764
  194.4 5.9 %copy-start.8 = (f32[40,512]{1,0:T(8,128)}, f32[40,512]{1,0:T(8,128)S(1)}, u32[]{:S(2)}) copy-start(f32[40,512]{1,0:T(8,128)S(1)} %collective-permute-done.12.refs_1_) | copy-start | bytes 245764
  200.3 0.6 copy-start.9
  200.3 0.7 copy-start.5
Sparse Core Ops, SparseCore 0:
  10.4 84.1 all-gather.2
  108.4 36.5 reduce-scatter.1
